TPU v7x, 256 devices: a whole 4x4x8 slice. The times are simulated.
256 devices in a mesh: seq: 16 (over z_lo, y, core), mlp: 16 (over x, z_hi).
Axes of the slice: x: 4, y: 4, z: 8 (z_hi: 4, z_lo: 2; z = z_hi * 2 + z_lo), core: 2. Of those that a mesh axis runs over, the one named last changes fastest.
Arguments:
- txt_q: bfloat16 [512, 2048], replicated, may hold values from -6 to 6
- txt_k: bfloat16 [512, 2048], replicated, may hold values from -6 to 6
- txt_v: bfloat16 [512, 2048], replicated, may hold values from -6 to 6
- txt_grad: bfloat16 [512, 2048], replicated, may hold values from -6 to 6
- img_q: bfloat16 [4096, 2048], P(('seq', 'mlp')), may hold values from -300 to 300
- img_k: bfloat16 [4096, 2048], P(('seq', 'mlp')), may hold values from -6 to 6
- img_v: bfloat16 [4096, 2048], P(('seq', 'mlp')), may hold values from -6 to 6
- img_grad: bfloat16 [4096, 2048], P(('seq', 'mlp')), may hold values from -6 to 6
Outputs:
- img_dq: float32 [4096, 2048], P(('seq', 'mlp'))
- img_dk: float32 [4096, 2048], P(('seq', 'mlp'))
- img_dv: float32 [4096, 2048], P(('seq', 'mlp'))
- txt_dq: float32 [512, 2048], P('mlp', 'seq')
- txt_dk: float32 [512, 2048], P('mlp', 'seq')
- txt_dv: float32 [512, 2048], P('mlp', 'seq')
All inputs are finite; a program needn't handle non-finite values.
Results may differ from a plain program's by a relative error of at most 0.014.
Values may be sent and summed in bfloat16 or wider, within the bound.
A program may use at most 128 MiB of HBM per device.

v0:
```python
import jax
import jax.numpy as jnp
from jax import lax
from jax.sharding import PartitionSpec as P

HD = 128


def attend_block(queries, cotangent, all_keys, values, score_scale):
    scores = (
        jnp.einsum("qd,kd->qk", queries, all_keys, preferred_element_type=jnp.float32) * score_scale
    )
    weights = jnp.exp(scores - jnp.max(scores, axis=1, keepdims=True))
    weights = weights / jnp.sum(weights, axis=1, keepdims=True)
    rounded = weights.astype(jnp.bfloat16)
    dprob = jnp.einsum("qd,kd->qk", cotangent, values, preferred_element_type=jnp.float32)
    delta = jnp.sum(weights * dprob, axis=1, keepdims=True)
    dscore = (weights * (dprob - delta)).astype(jnp.bfloat16)
    d_query = (
        jnp.einsum("qk,kd->qd", dscore, all_keys, preferred_element_type=jnp.float32) * score_scale
    )
    d_key = (
        jnp.einsum("qk,qd->kd", dscore, queries, preferred_element_type=jnp.float32) * score_scale
    )
    d_value = jnp.einsum("qk,qd->kd", rounded, cotangent, preferred_element_type=jnp.float32)
    return (d_query, jnp.concatenate([d_key, d_value], axis=1))


def per_device(txt_q, txt_k, txt_v, txt_grad, img_q, img_k, img_v, img_grad):
    head_width = HD
    score_scale = head_width ** (-0.5)
    head_index = lax.axis_index("seq")
    member = lax.axis_index("mlp")
    groups = lax.axis_size("mlp")
    text_total = txt_q.shape[0]
    text_rows = text_total // groups
    text_start = member * text_rows

    def head_cols(array):
        return lax.dynamic_slice_in_dim(array, head_index * head_width, head_width, 1)

    def own_rows(array):
        return lax.dynamic_slice_in_dim(array, text_start, text_rows, 0)

    head_k = head_cols(txt_k)
    head_v = head_cols(txt_v)
    own_q = own_rows(head_cols(txt_q))
    own_g = own_rows(head_cols(txt_grad))
    local_q, local_k, local_v, local_g = (
        lax.all_to_all(img_q, "seq", split_axis=1, concat_axis=0, tiled=True),
        lax.all_to_all(img_k, "seq", split_axis=1, concat_axis=0, tiled=True),
        lax.all_to_all(img_v, "seq", split_axis=1, concat_axis=0, tiled=True),
        lax.all_to_all(img_grad, "seq", split_axis=1, concat_axis=0, tiled=True),
    )
    far_keys, far_values = (
        lax.all_gather(local_k, "mlp", axis=0, tiled=True),
        lax.all_gather(local_v, "mlp", axis=0, tiled=True),
    )
    all_keys = jnp.concatenate([head_k, far_keys], axis=0)
    values = jnp.concatenate([head_v, far_values], axis=0)
    image_rows = local_q.shape[0]
    half_rows = image_rows // 2
    blocks = [
        (own_q, own_g),
        (local_q[:half_rows], local_g[:half_rows]),
        (local_q[half_rows:], local_g[half_rows:]),
    ]
    query_grads = []
    key_terms = None
    for query_rows, cot_rows in blocks:
        d_query, term = attend_block(query_rows, cot_rows, all_keys, values, score_scale)
        query_grads.append(d_query)
        key_terms = term if key_terms is None else key_terms + term
    text_dq = query_grads[0]
    image_dq = jnp.concatenate(query_grads[1:], axis=0)
    summed = lax.psum(key_terms[:text_total], "mlp")
    text_grads = lax.dynamic_slice_in_dim(summed, text_start, text_rows, 0)
    scatter_terms = key_terms[text_total:]
    owned = lax.psum_scatter(scatter_terms, "mlp", scatter_dimension=0, tiled=True)
    out_dq, out_dk, out_dv = (
        lax.all_to_all(image_dq, "seq", split_axis=0, concat_axis=1, tiled=True),
        lax.all_to_all(owned[:, :head_width], "seq", split_axis=0, concat_axis=1, tiled=True),
        lax.all_to_all(owned[:, head_width:], "seq", split_axis=0, concat_axis=1, tiled=True),
    )
    return (out_dq, out_dk, out_dv, text_dq, text_grads[:, :head_width], text_grads[:, head_width:])


def solution(mesh):
    placed = (
        P(),
        P(),
        P(),
        P(),
        P(("seq", "mlp"), None),
        P(("seq", "mlp"), None),
        P(("seq", "mlp"), None),
        P(("seq", "mlp"), None),
    )
    return jax.shard_map(
        per_device,
        mesh=mesh,
        in_specs=placed,
        out_specs=(
            P(("seq", "mlp"), None),
            P(("seq", "mlp"), None),
            P(("seq", "mlp"), None),
            P("mlp", "seq"),
            P("mlp", "seq"),
            P("mlp", "seq"),
        ),
        check_vma=False,
    )
```

profile of v0, /device:TPU:1, one launch (start us, length us, event | category | flops | bytes accessed | tf_op | source)
XLA Modules:
  0.0 427.1 jit_solution(7907193972285797965)
XLA Ops:
  7.2 0.0 copy-start
  7.2 0.0 all-gather.3.cloned.1.call-start
  7.2 1.0 copy_bitcast_fusion.6
  8.2 13.1 %all_to_all.127 = bf16[16,16,128]{2,0,1:T(8,128)(2,1)} all-to-all(bf16[16,16,128]{2,0,1:T(8,128)(2,1)S(1)} %copy_bitcast_fusion.6), channel_id=1, replica_groups=mesh['seq'=16,'mlp'=16] {'seq'}, dimensions={1} | all-to-all | bytes 131072 | tf_op jit(solution)/shard_map/all_to_all | solution.py:51
  21.3 0.0 all-gather.3.cloned.1.call-update
  21.3 0.0 all-gather.5.cloned.1.call-start
  21.4 0.9 copy_bitcast_fusion.4
  22.2 9.4 %all_to_all.128 = bf16[16,16,128]{2,0,1:T(8,128)(2,1)} all-to-all(bf16[16,16,128]{2,0,1:T(8,128)(2,1)S(1)} %copy_bitcast_fusion.4), channel_id=1, replica_groups=mesh['seq'=16,'mlp'=16] {'seq'}, dimensions={1} | all-to-all | bytes 131072 | tf_op jit(solution)/shard_map/all_to_all | solution.py:52
  31.6 0.0 all-gather.5.cloned.1.call-update
  31.7 1.5 copy_bitcast_fusion.5
  33.1 3.7 all-to-all-start.1
  36.9 1.5 copy_bitcast_fusion.3
  38.3 0.9 constant_dynamic-slice_fusion.2
  39.3 1.6 constant_dynamic-slice_fusion.1
  40.9 1.9 all-to-all-done.1
  42.8 3.9 all-to-all-start.3
  46.7 0.0 reduce-scatter.2.cloned.1.call-start
  46.8 5.8 %all-to-all-done.3 = bf16[16,16,128]{2,0,1:T(8,128)(2,1)S(1)} async-done(((bf16[16,16,128]{2,0,1:T(8,128)(2,1)}), bf16[16,16,128]{2,0,1:T(8,128)(2,1)S(1)}, u32[]{:S(2)}, u32[]{:S(2)}) %all-to-all-start.3) | async-done | bytes 65568 | tf_op jit(solution)/shard_map/all_to_all | solution.py:53
  52.5 21.1 %all-gather.3.cloned.1.call-done = bf16[4096,128]{1,0:T(8,128)(2,1)} async-done(((bf16[256,128]{1,0:T(8,128)(2,1)}), bf16[4096,128]{1,0:T(8,128)(2,1)}) %all-gather.3.cloned.1.call-update) | async-done | bytes 1048592 | tf_op jit(solution)/shard_map/all_gather | solution.py:56
  73.6 1.9 fusion.32
  75.5 0.3 fusion.12
  75.8 2.1 fusion.14
  77.9 49.0 %all-gather.5.cloned.1.call-done = bf16[4096,128]{1,0:T(8,128)(2,1)} async-done(((bf16[256,128]{1,0:T(8,128)(2,1)}), bf16[4096,128]{1,0:T(8,128)(2,1)}) %all-gather.5.cloned.1.call-update) | async-done | bytes 1048592 | tf_op jit(solution)/shard_map/all_gather | solution.py:57
  126.8 1.9 multiply_reduce_fusion
  128.7 0.2 multiply_convert_fusion
  128.9 1.5 convolution_multiply_fusion
  130.4 0.8 fusion.30
  131.2 0.6 fusion.8
  131.9 0.5 fusion.10
  132.4 0.4 copy-done.15
  132.8 0.4 copy-done.16
  133.2 0.8 fusion.1
  134.0 0.6 fusion.2
  134.6 0.4 convolution_multiply_fusion.1
  135.0 0.8 fusion.31
  135.8 0.6 fusion.6
  136.5 0.5 fusion.9
  137.0 0.8 fusion.3
  137.8 0.6 fusion.4
  138.4 1.0 copy-done.7
  139.4 0.5 convolution_multiply_fusion.2
  139.9 1.2 copy-done.1
  141.1 0.7 fusion
  141.8 0.9 copy-done.4
  142.7 2.2 slice.60
  144.9 0.0 reduce-scatter.2.cloned.1.call-update
  145.0 1.9 convolution_multiply_fusion.6
  146.9 0.5 convolution_multiply_fusion.7
  147.4 0.7 pad_maximum_fusion.5
  148.1 6.5 %all-to-all-start.4 = ((f32[16,16,128]{2,1,0:T(8,128)}), f32[16,16,128]{2,1,0:T(8,128)}, u32[]{:S(2)}, u32[]{:S(2)}) async-start(f32[16,16,128]{2,1,0:T(8,128)} %bitcast.14), calls=%async_computation.4 | async-start | bytes 262144 | tf_op jit(solution)/shard_map/all_to_all | solution.py:81
  154.6 0.0 all-reduce.2.cloned.1.call-start
  154.6 2.5 maximum_add_fusion.1
  157.1 0.0 all-reduce.2.cloned.1.call-update
  157.1 1.8 convolution_multiply_fusion.8
  159.0 80.0 %reduce-scatter.2.cloned.1.call-done = f32[256,256]{1,0:T(8,128)} async-done(((f32[4096,256]{1,0:T(8,128)}), f32[256,256]{1,0:T(8,128)}) %reduce-scatter.2.cloned.1.call-update) | async-done | bytes 262160 | tf_op jit(solution)/shard_map/reduce_scatter | solution.py:79
  238.9 1.7 fusion.27
  240.6 5.6 %all-to-all-start.5 = ((f32[16,16,128]{2,1,0:T(8,128)}), f32[16,16,128]{2,1,0:T(8,128)S(1)}, u32[]{:S(2)}, u32[]{:S(2)}) async-start(f32[16,16,128]{2,1,0:T(8,128)} %bitcast.16), calls=%async_computation.6 | async-start | bytes 262144 | tf_op jit(solution)/shard_map/all_to_all | solution.py:82
  246.2 1.6 copy_bitcast_fusion.2
  247.7 148.9 %all-reduce.2.cloned.1.call-done = f32[512,256]{1,0:T(8,128)} async-done(((f32[512,256]{1,0:T(8,128)}), f32[512,256]{1,0:T(8,128)}) %all-reduce.2.cloned.1.call-update) | async-done | bytes 524304 | tf_op jit(solution)/shard_map/psum | solution.py:76
  396.6 1.3 fusion.26
  397.9 15.8 %all-to-all-start.6 = ((f32[16,16,128]{2,1,0:T(8,128)}), f32[16,16,128]{2,1,0:T(8,128)S(1)}, u32[]{:S(2)}, u32[]{:S(2)}) async-start(f32[16,16,128]{2,1,0:T(8,128)} %bitcast.18), calls=%async_computation.7 | async-start | bytes 262144 | tf_op jit(solution)/shard_map/all_to_all | solution.py:83
  413.7 0.7 copy_bitcast_fusion.1
  414.4 5.5 %all-to-all-done.6 = f32[16,16,128]{2,1,0:T(8,128)S(1)} async-done(((f32[16,16,128]{2,1,0:T(8,128)}), f32[16,16,128]{2,1,0:T(8,128)S(1)}, u32[]{:S(2)}, u32[]{:S(2)}) %all-to-all-start.6) | async-done | bytes 131104 | tf_op jit(solution)/shard_map/all_to_all | solution.py:83
  419.9 0.7 copy_bitcast_fusion
  (32 shorter events, 0.1 us)
Async XLA Ops:
  7.2 68.6 %copy-start = (bf16[512,2048]{1,0:T(8,128)(2,1)S(1)}, bf16[512,2048]{1,0:T(8,128)(2,1)}, u32[]{:S(2)}) copy-start(bf16[512,2048]{1,0:T(8,128)(2,1)} %param.11) | copy-start | bytes 6291460
  7.2 66.4 %all-gather.3.cloned.1.call-start = ((), (), s32[]{:S(2)}) async-start(), calls=%async_computation.8 | async-start | bytes 1114112 | tf_op jit(solution)/shard_map/all_gather | solution.py:56
  21.3 105.5 %all-gather.5.cloned.1.call-start = ((), (), s32[]{:S(2)}) async-start(), calls=%async_computation.9 | async-start | bytes 1114112 | tf_op jit(solution)/shard_map/all_gather | solution.py:57
  33.1 9.6 %all-to-all-start.1 = ((bf16[16,16,128]{2,0,1:T(8,128)(2,1)}), bf16[16,16,128]{2,0,1:T(8,128)(2,1)S(1)}, u32[]{:S(2)}, u32[]{:S(2)}) async-start(bf16[16,16,128]{2,0,1:T(8,128)(2,1)} %copy_bitcast_fusion.5), calls=%async_computation.1 | async-start | bytes 131072 | tf_op jit(solution)/shard_map/all_to_all | solution.py:50
  39.3 107.6 %copy-start.14 = (bf16[512,128]{1,0:T(8,128)(2,1)}, bf16[512,128]{1,0:T(8,128)(2,1)S(1)}, u32[]{:S(2)}) copy-start(bf16[512,128]{1,0:T(8,128)(2,1)S(1)} %constant_dynamic-slice_fusion.2) | copy-start | bytes 393220
  42.8 9.8 %all-to-all-start.3 = ((bf16[16,16,128]{2,0,1:T(8,128)(2,1)}), bf16[16,16,128]{2,0,1:T(8,128)(2,1)S(1)}, u32[]{:S(2)}, u32[]{:S(2)}) async-start(bf16[16,16,128]{2,0,1:T(8,128)(2,1)} %copy_bitcast_fusion.3), calls=%async_computation.3 | async-start | bytes 131072 | tf_op jit(solution)/shard_map/all_to_all | solution.py:53
  46.7 192.2 %reduce-scatter.2.cloned.1.call-start = ((), (), s32[]{:S(2)}) async-start(), calls=%async_computation.10 | async-start | bytes 4456448 | tf_op jit(solution)/shard_map/reduce_scatter | solution.py:79
  128.7 1.7 copy-start.9
  128.9 2.3 copy-start.12
  130.4 9.5 %copy-start.2 = (f32[4608,128]{1,0:T(8,128)}, f32[4608,128]{1,0:T(8,128)S(1)}, u32[]{:S(2)}) copy-start(f32[4608,128]{1,0:T(8,128)S(1)} %convolution_multiply_fusion) | copy-start | bytes 7077892
  131.9 0.9 copy-start.15
  131.9 1.3 copy-start.16
  133.2 6.7 %copy-start.5 = (f32[4608,128]{1,0:T(8,128)}, f32[4608,128]{1,0:T(8,128)S(1)}, u32[]{:S(2)}) copy-start(f32[4608,128]{1,0:T(8,128)S(1)} %fusion.10) | copy-start | bytes 7077892
  135.0 4.9 %copy-start.3 = (f32[4608,128]{1,0:T(8,128)}, f32[4608,128]{1,0:T(8,128)S(1)}, u32[]{:S(2)}) copy-start(f32[4608,128]{1,0:T(8,128)S(1)} %convolution_multiply_fusion.1) | copy-start | bytes 7077892
  137.0 2.9 copy-start.6
  138.4 1.0 copy-start.7
  139.4 1.7 copy-start.1
  141.1 1.6 copy-start.4
  144.9 1.9 copy-start.8
  145.0 1.9 copy-start.10
  148.1 92.5 %all-to-all-start.4 = ((f32[16,16,128]{2,1,0:T(8,128)}), f32[16,16,128]{2,1,0:T(8,128)}, u32[]{:S(2)}, u32[]{:S(2)}) async-start(f32[16,16,128]{2,1,0:T(8,128)} %bitcast.14), calls=%async_computation.4 | async-start | bytes 262144 | tf_op jit(solution)/shard_map/all_to_all | solution.py:81
  154.5 2.6 copy-start.11
  154.5 2.6 copy-start.13
  154.6 242.0 %all-reduce.2.cloned.1.call-start = ((), (), s32[]{:S(2)}) async-start(), calls=%async_computation.11 | async-start | bytes 1048576 | tf_op jit(solution)/shard_map/psum | solution.py:76
  240.6 157.3 %all-to-all-start.5 = ((f32[16,16,128]{2,1,0:T(8,128)}), f32[16,16,128]{2,1,0:T(8,128)S(1)}, u32[]{:S(2)}, u32[]{:S(2)}) async-start(f32[16,16,128]{2,1,0:T(8,128)} %bitcast.16), calls=%async_computation.6 | async-start | bytes 262144 | tf_op jit(solution)/shard_map/all_to_all | solution.py:82
  397.9 21.9 %all-to-all-start.6 = ((f32[16,16,128]{2,1,0:T(8,128)}), f32[16,16,128]{2,1,0:T(8,128)S(1)}, u32[]{:S(2)}, u32[]{:S(2)}) async-start(f32[16,16,128]{2,1,0:T(8,128)} %bitcast.18), calls=%async_computation.7 | async-start | bytes 262144 | tf_op jit(solution)/shard_map/all_to_all | solution.py:83
Sparse Core Ops, SparseCore 0:
  21.4 52.1 all-gather.2
  76.1 50.7 all-gather.4
  145.1 93.7 reduce-scatter.1
  241.6 154.9 all-reduce.1
where the time goes:
time: 428 us; the launch traced here: 427 us
  waiting for transfers between devices  312 us (73%)
  starting transfers between devices  35.6 us (8%)
  blocking collectives  22.5 us (5%)
  local copies, waits for them, and re-layouts  19.5 us (5%)
  matrix products  16.6 us (4%)
  between operations  14.1 us (3%)
  other arithmetic  6.79 us (2%)
    psum x1, waiting for transfers between devices, per_device(): summed = lax.psum(key_terms[:text_total], 'mlp')  149 us
    reduce_scatter x1, waiting for transfers between devices, per_device(): lax.psum_scatter(scatter_terms, 'mlp', scatter_dimension=0, tiled=True)  80 us
    all_gather x1, waiting for transfers between devices, per_device(): lax.all_gather(local_v, 'mlp', axis=0, tiled=True)  49 us
    all_gather x1, waiting for transfers between devices, per_device(): lax.all_gather(local_k, 'mlp', axis=0, tiled=True)  21.1 us
    all_to_all x1, starting transfers between devices, per_device(): lax.all_to_all(owned[:, head_width:], 'seq', split_axis=0, concat_axis=1,...  15.8 us
    all_to_all x1, blocking collectives, per_device(): lax.all_to_all(img_k, 'seq', split_axis=1, concat_axis=0, tiled=True)  13.1 us
    all_to_all x1, blocking collectives, per_device(): lax.all_to_all(img_v, 'seq', split_axis=1, concat_axis=0, tiled=True)  9.42 us
  transfers between devices with their start and end apart: 9, of which 7 were waited for; matrix products, arithmetic and copies ran while one was open for 5% of the time, Pallas kernels for 0%

commit v1 on v0

v1 whole, which is shorter than its diff:
```python
import jax
import jax.numpy as jnp
from jax import lax
from jax.experimental import pallas as pl
from jax.experimental.pallas import tpu as pltpu
from jax.sharding import PartitionSpec as P

HD = 128
LOG2E = 1.4426950408889634
SCALE = HD ** -0.5
BF = jnp.bfloat16
F32 = jnp.float32
MESH = pl.DeviceIdType.MESH

START = (0, 128, 384, 640, 896)
SIZE = (128, 256, 256, 256, 256)
ROWS = 1152


def nt(a, b):
    return lax.dot_general(a, b, (((1,), (1,)), ((), ())), preferred_element_type=F32)


def nn(a, b):
    return lax.dot_general(a, b, (((1,), (0,)), ((), ())), preferred_element_type=F32)


def body(
    tq, tk, tv, tg, iq, ik, iv, ig,
    oq, ok, ov, otq, otk, otv,
    flat, stage, own, qg, kv, text,
    qall, kall, vall, gall, ktall,
    e_buf, dp_buf, pb_buf, ds_buf, mx, sm, dl, st, st_in,
    dkv_st, dkv_in, dkvt_st, dkvt_in, dkv_own, dkvt_own,
    dq_st, dq_in, dqt_st, dqt_in, dq_own, dqt_own, dq_text,
    out_st, fin, tout, tfin,
    in_sem, text_sem,
    p1_s, p1_r, qg_s, qg_r, kv_s, kv_r, st_s, st_r,
    dkv_s, dkv_r, dkvt_s, dkvt_r, dq_s, dq_r, dqt_s, dqt_r,
    p4_s, p4_r, tx_s, tx_r,
):
    s = lax.axis_index("seq")
    m = lax.axis_index("mlp")
    z0, y, core = s // 8, (s // 2) % 4, s % 2
    x, zh = m // 4, m % 4

    def flip(j):
        zf = 1 - z0 if j & 2 else z0
        cf = 1 - core if j & 1 else core
        return zf * 8 + y * 2 + cf

    def turn(j):
        return z0 * 8 + ((y + j) % 4) * 2 + core

    def around(i, sign):
        dz, dx = i // 4, i % 4
        return ((x + sign * dx + 4) % 4) * 4 + (zh + sign * dz + 4) % 4

    loads = []
    for n, ref in enumerate((iq, ig, ik, iv)):
        c = pltpu.make_async_copy(ref, flat.at[n], in_sem.at[n])
        c.start()
        loads.append(c)
    col = pl.ds(pl.multiple_of(m * HD, HD), HD)
    tloads = []
    for n, ref in enumerate((tq, tg, tk, tv)):
        for j in range(4):
            owner = (j // 2) * 8 + y * 2 + j % 2 if n < 2 else turn((4 - j) % 4)
            rows = pl.ds(pl.multiple_of(owner * 32, 32), 32)
            c = pltpu.make_async_copy(ref.at[rows, col], text.at[n, pl.ds(j * 32, 32)], text_sem.at[n, j])
            c.start()
            tloads.append(c)

    barrier = pltpu.get_barrier_semaphore()
    for j in range(1, 4):
        pl.semaphore_signal(barrier, inc=1, device_id={"seq": flip(j), "mlp": m}, device_id_type=MESH)
        pl.semaphore_signal(barrier, inc=1, device_id={"seq": turn(j), "mlp": m}, device_id_type=MESH)
    for i in range(1, 16):
        pl.semaphore_signal(barrier, inc=1, device_id={"seq": s, "mlp": around(i, 1)}, device_id_type=MESH)

    @pl.when(s != m)
    def _():
        pl.semaphore_signal(barrier, inc=1, device_id={"seq": m, "mlp": s}, device_id_type=MESH)
        pl.semaphore_wait(barrier, 22)

    @pl.when(s == m)
    def _():
        pl.semaphore_wait(barrier, 21)

    for c in loads:
        c.wait()
    for h in range(16):
        for n in range(4):
            stage[h, n] = flat[n, :, h * HD:(h + 1) * HD]

    sends = []
    for i in (8, 9, 11, 10, 4, 12, 5, 13, 7, 15, 6, 14, 1, 3, 2):
        dest = around(i, -1)
        c = pltpu.make_async_remote_copy(
            stage.at[dest], own.at[i], p1_s.at[i], p1_r.at[i],
            device_id={"seq": s, "mlp": dest}, device_id_type=MESH)
        c.start()
        sends.append(c)
    own[0] = stage[m]

    for c in tloads:
        c.wait()
    qall[0:128] = text[0]
    gall[0:128] = text[1]
    kall[0:128] = text[2]
    vall[0:128] = text[3]

    for g in range(4):
        for i in range(4 * g, 4 * g + 4):
            if i:
                pltpu.make_async_copy(own.at[i], own.at[i], p1_r.at[i]).wait()
        part = pl.ds(4 * g, 4)
        for j in (2, 3, 1):
            c = pltpu.make_async_remote_copy(
                own.at[part, pl.ds(0, 2)], qg.at[j - 1, part], qg_s.at[g, j - 1], qg_r.at[g, j - 1],
                device_id={"seq": flip(j), "mlp": m}, device_id_type=MESH)
            c.start()
            sends.append(c)
        for j in (2, 1, 3):
            c = pltpu.make_async_remote_copy(
                own.at[part, pl.ds(2, 2)], kv.at[j - 1, part], kv_s.at[g, j - 1], kv_r.at[g, j - 1],
                device_id={"seq": turn(j), "mlp": m}, device_id_type=MESH)
            c.start()
            sends.append(c)

    qall[128:384] = own[:, 0].reshape(256, HD)
    gall[128:384] = own[:, 1].reshape(256, HD)
    kall[128:384] = own[:, 2].reshape(256, HD)
    vall[128:384] = own[:, 3].reshape(256, HD)

    def pass_one(kc, qc):
        kr, qr = pl.ds(START[kc], SIZE[kc]), pl.ds(START[qc], SIZE[qc])
        scores = nt(kall[kr], qall[qr])
        top = jnp.max(scores, axis=0, keepdims=True)
        e = jnp.exp2((scores - top) * (SCALE * LOG2E))
        dp = nt(vall[kr], gall[qr])
        mx[kc:kc + 1, qr] = top
        sm[kc:kc + 1, qr] = jnp.sum(e, axis=0, keepdims=True)
        dl[kc:kc + 1, qr] = jnp.sum(e * dp, axis=0, keepdims=True)
        e_buf[kr, qr] = e
        dp_buf[kr, qr] = dp

    have_k, have_q = [0, 1], [0, 1]
    for kc in have_k:
        for qc in have_q:
            pass_one(kc, qc)
    for kind, j in (("q", 1), ("k", 1), ("k", 3), ("q", 2), ("k", 2), ("q", 3)):
        r = pl.ds(START[j + 1], 256)
        sem, buf, left, right = (qg_r, qg, qall, gall) if kind == "q" else (kv_r, kv, kall, vall)
        for g in range(4):
            piece = buf.at[j - 1, pl.ds(4 * g, 4)]
            pltpu.make_async_copy(piece, piece, sem.at[g, j - 1]).wait()
        left[r] = buf[j - 1, :, 0].reshape(256, HD)
        right[r] = buf[j - 1, :, 1].reshape(256, HD)
        if kind == "q":
            for kc in have_k:
                pass_one(kc, j + 1)
            have_q.append(j + 1)
        else:
            for qc in have_q:
                pass_one(j + 1, qc)
            have_k.append(j + 1)

    unit = SCALE * LOG2E
    top = jnp.max(mx[0:5], axis=0, keepdims=True)
    w = jnp.exp2((mx[0:5] - top) * unit)
    total = jnp.sum(w * sm[0:5], axis=0, keepdims=True)
    dsum = jnp.sum(w * dl[0:5], axis=0, keepdims=True)
    for b in range(9):
        cols = slice(b * 128, (b + 1) * 128)
        st[b:b + 1] = top[:, cols]
        st[9 + b:10 + b] = total[:, cols]
        st[18 + b:19 + b] = dsum[:, cols]
    for j in (2, 3, 1):
        c = pltpu.make_async_remote_copy(
            st, st_in.at[j - 1], st_s.at[j - 1], st_r.at[j - 1],
            device_id={"seq": flip(j), "mlp": m}, device_id_type=MESH)
        c.start()
        sends.append(c)
    ktall[...] = kall[...].T
    for j in (1, 2, 3):
        pltpu.make_async_copy(st_in.at[j - 1], st_in.at[j - 1], st_r.at[j - 1]).wait()

    def theirs(j, first):
        rows = [0] + [1 + 2 * (r ^ j) + half for r in range(4) for half in range(2)]
        return jnp.concatenate([st_in[j - 1, first + b:first + b + 1] for b in rows], axis=0)

    tops = [st[0:9]] + [theirs(j, 0) for j in (1, 2, 3)]
    sums = [st[9:18]] + [theirs(j, 9) for j in (1, 2, 3)]
    dsums = [st[18:27]] + [theirs(j, 18) for j in (1, 2, 3)]
    gtop = jnp.maximum(jnp.maximum(tops[0], tops[1]), jnp.maximum(tops[2], tops[3]))
    ws = [jnp.exp2((t - gtop) * unit) for t in tops]
    gsum = ws[0] * sums[0] + ws[1] * sums[1] + ws[2] * sums[2] + ws[3] * sums[3]
    gd = ws[0] * dsums[0] + ws[1] * dsums[1] + ws[2] * dsums[2] + ws[3] * dsums[3]
    inv = 1.0 / gsum
    delta = gd * inv

    def as_row(a):
        return jnp.concatenate([a[b:b + 1] for b in range(9)], axis=1)

    gtop_row, inv_row, delta_row = as_row(gtop), as_row(inv), as_row(delta)
    mx[0:5] = jnp.exp2((mx[0:5] - gtop_row) * unit) * inv_row
    dl[0:1] = delta_row

    for kc in (3, 2, 4, 0, 1):
        kr = pl.ds(START[kc], SIZE[kc])
        for qc in range(5):
            qr = pl.ds(START[qc], SIZE[qc])
            p = e_buf[kr, qr] * mx[kc:kc + 1, qr]
            pb_buf[kr, qr] = p.astype(BF)
            ds_buf[kr, qr] = (p * (dp_buf[kr, qr] - dl[0:1, qr])).astype(BF)
        dk = nn(ds_buf[kr], qall[...]) * SCALE
        dv = nn(pb_buf[kr], gall[...])
        if kc >= 2:
            j = kc - 1
            dkv_st[j - 1, 0] = dk.astype(BF)
            dkv_st[j - 1, 1] = dv.astype(BF)
            c = pltpu.make_async_remote_copy(
                dkv_st.at[j - 1], dkv_in.at[j - 1], dkv_s.at[j - 1], dkv_r.at[j - 1],
                device_id={"seq": turn(4 - j), "mlp": m}, device_id_type=MESH)
            c.start()
            sends.append(c)
        elif kc == 0:
            for j in range(4):
                part = slice(j * 32, j * 32 + 32)
                if j == 0:
                    dkvt_own[0] = dk[part]
                    dkvt_own[1] = dv[part]
                else:
                    dkvt_st[j - 1, 0] = dk[part].astype(BF)
                    dkvt_st[j - 1, 1] = dv[part].astype(BF)
                    c = pltpu.make_async_remote_copy(
                        dkvt_st.at[j - 1], dkvt_in.at[j - 1], dkvt_s.at[j - 1], dkvt_r.at[j - 1],
                        device_id={"seq": turn(4 - j), "mlp": m}, device_id_type=MESH)
                    c.start()
                    sends.append(c)
        else:
            dkv_own[0] = dk
            dkv_own[1] = dv

    for qc in (3, 4, 2, 0, 1):
        qr = pl.ds(START[qc], SIZE[qc])
        dqt = nn(ktall[...], ds_buf[:, qr]) * SCALE
        if qc >= 2:
            j = qc - 1
            dq_st[j - 1] = dqt.astype(BF)
            c = pltpu.make_async_remote_copy(
                dq_st.at[j - 1], dq_in.at[j - 1], dq_s.at[j - 1], dq_r.at[j - 1],
                device_id={"seq": flip(j), "mlp": m}, device_id_type=MESH)
            c.start()
            sends.append(c)
        elif qc == 0:
            dq_text[...] = dqt.T
            for j in range(4):
                peer = flip(j)
                part = pl.ds(pl.multiple_of((peer // 8 * 2 + peer % 2) * 32, 32), 32)
                if j == 0:
                    dqt_own[...] = dq_text[part]
                else:
                    dqt_st[j - 1] = dq_text[part].astype(BF)
                    c = pltpu.make_async_remote_copy(
                        dqt_st.at[j - 1], dqt_in.at[j - 1], dqt_s.at[j - 1], dqt_r.at[j - 1],
                        device_id={"seq": flip(j), "mlp": m}, device_id_type=MESH)
                    c.start()
                    sends.append(c)
        else:
            dq_own[...] = dqt

    def arrived(buf, sem):
        for j in range(3):
            pltpu.make_async_copy(buf.at[j], buf.at[j], sem.at[j]).wait()

    def plus(own_term, buf, *at):
        t = own_term
        for j in range(3):
            t = t + buf[(j, *at)].astype(F32)
        return t

    arrived(dkv_in, dkv_r)
    out_st[:, 1] = plus(dkv_own[0], dkv_in, 0).astype(BF).reshape(16, 16, HD)
    out_st[:, 2] = plus(dkv_own[1], dkv_in, 1).astype(BF).reshape(16, 16, HD)
    arrived(dq_in, dq_r)
    out_st[:, 0] = plus(dq_own[...], dq_in).T.astype(BF).reshape(16, 16, HD)
    for i in (8, 9, 11, 10, 4, 12, 5, 13, 7, 15, 6, 14, 1, 3, 2):
        dest = around(i, 1)
        c = pltpu.make_async_remote_copy(
            out_st.at[i], fin.at[m], p4_s.at[i], p4_r.at[i],
            device_id={"seq": s, "mlp": dest}, device_id_type=MESH)
        c.start()
        sends.append(c)
    fin[m] = out_st[0]

    arrived(dkvt_in, dkvt_r)
    arrived(dqt_in, dqt_r)
    tout[0] = plus(dqt_own[...], dqt_in).astype(BF)
    tout[1] = plus(dkvt_own[0], dkvt_in, 0).astype(BF)
    tout[2] = plus(dkvt_own[1], dkvt_in, 1).astype(BF)

    @pl.when(s != m)
    def _():
        c = pltpu.make_async_remote_copy(
            tout, tfin, tx_s, tx_r, device_id={"seq": m, "mlp": s}, device_id_type=MESH)
        c.start()
        c.wait()

    @pl.when(s == m)
    def _():
        tfin[...] = tout[...]

    otq[...] = tfin[0].astype(F32)
    otk[...] = tfin[1].astype(F32)
    otv[...] = tfin[2].astype(F32)

    for i in range(1, 16):
        piece = fin.at[around(i, -1)]
        pltpu.make_async_copy(piece, piece, p4_r.at[i]).wait()
    for h in range(16):
        cols = slice(h * HD, (h + 1) * HD)
        oq[:, cols] = fin[h, 0].astype(F32)
        ok[:, cols] = fin[h, 1].astype(F32)
        ov[:, cols] = fin[h, 2].astype(F32)
    for c in sends:
        c.wait_send()


def per_device(*args):
    anyspace = pl.BlockSpec(memory_space=pl.ANY)
    vmem = pl.BlockSpec(memory_space=pltpu.VMEM)
    sem = pltpu.SemaphoreType.DMA
    V = pltpu.VMEM
    return pl.pallas_call(
        body,
        out_shape=[jax.ShapeDtypeStruct((16, 2048), F32)] * 3 + [jax.ShapeDtypeStruct((32, HD), F32)] * 3,
        in_specs=[anyspace] * 8,
        out_specs=[vmem] * 6,
        scratch_shapes=[
            V((4, 16, 2048), BF), V((16, 4, 16, HD), BF), V((16, 4, 16, HD), BF),
            V((3, 16, 2, 16, HD), BF), V((3, 16, 2, 16, HD), BF), V((4, 128, HD), BF),
            V((ROWS, HD), BF), V((ROWS, HD), BF), V((ROWS, HD), BF), V((ROWS, HD), BF), V((HD, ROWS), BF),
            V((ROWS, ROWS), F32), V((ROWS, ROWS), F32), V((ROWS, ROWS), BF), V((ROWS, ROWS), BF),
            V((8, ROWS), F32), V((8, ROWS), F32), V((8, ROWS), F32), V((32, HD), F32), V((3, 32, HD), F32),
            V((3, 2, 256, HD), BF), V((3, 2, 256, HD), BF), V((3, 2, 32, HD), BF), V((3, 2, 32, HD), BF),
            V((2, 256, HD), F32), V((2, 32, HD), F32),
            V((3, HD, 256), BF), V((3, HD, 256), BF), V((3, 32, HD), BF), V((3, 32, HD), BF),
            V((HD, 256), F32), V((32, HD), F32), V((HD, HD), F32),
            V((16, 3, 16, HD), BF), V((16, 3, 16, HD), BF), V((3, 32, HD), BF), V((3, 32, HD), BF),
            sem((4,)), sem((4, 4)),
            sem((16,)), sem((16,)), sem((4, 3)), sem((4, 3)), sem((4, 3)), sem((4, 3)), sem((3,)), sem((3,)),
            sem((3,)), sem((3,)), sem((3,)), sem((3,)), sem((3,)), sem((3,)), sem((3,)), sem((3,)),
            sem((16,)), sem((16,)), sem, sem,
        ],
        compiler_params=pltpu.CompilerParams(
            collective_id=0, has_side_effects=True, vmem_limit_bytes=50 * 1024 * 1024),
        cost_estimate=pl.CostEstimate(flops=1_700_000_000, bytes_accessed=2_000_000, transcendentals=1_300_000),
    )(*args)


def solution(mesh):
    tokens = P(("seq", "mlp"), None)
    return jax.shard_map(
        per_device,
        mesh=mesh,
        in_specs=(P(), P(), P(), P(), tokens, tokens, tokens, tokens),
        out_specs=(tokens, tokens, tokens, P("mlp", "seq"), P("mlp", "seq"), P("mlp", "seq")),
        check_vma=False,
    )
```

time: 428 us -> 60 us (0.14)
  waiting for transfers between devices: 312 us -> 0 us
  Pallas kernels: 0 us -> 50.3 us
  starting transfers between devices: 35.6 us -> 0 us
  blocking collectives: 22.5 us -> 0 us
  matrix products: 16.6 us -> 0 us
  between operations: 14.1 us -> 0.66 us
  local copies, waits for them, and re-layouts: 19.5 us -> 8.72 us
  other arithmetic: 6.79 us -> 0 us
    psum x1 -> x0, waiting for transfers between devices: 149 us -> none  [per_device(): summed = lax.psum(key_terms[:text_total], 'mlp')]
    reduce_scatter x1 -> x0, waiting for transfers between devices: 80 us -> none  [per_device(): lax.psum_scatter(scatter_terms, 'mlp', scatter_dimension=0, tiled=True)]
    all_gather x2 -> x0, waiting for transfers between devices: 70.1 us -> none  [the longest x1 49 us: per_device(): lax.all_gather(local_v, 'mlp', axis=0, tiled=True)]
    pallas_call x0 -> x1, Pallas kernels: none -> 50.3 us  [per_device(): pl.pallas_call(body, out_shape=[jax.ShapeDtypeStruct((16, 2048), F32)] *...]
    all_to_all x5 -> x0, starting transfers between devices: 35.5 us -> none  [the longest x1 15.8 us: per_device(): lax.all_to_all(owned[:, head_width:], 'seq', split_axis=0, concat_axis=1,...]
    all_to_all x2 -> x0, blocking collectives: 22.5 us -> none  [the longest x1 13.1 us: per_device(): lax.all_to_all(img_k, 'seq', split_axis=1, concat_axis=0, tiled=True)]
    dot_general x15 -> x0, matrix products: 16.6 us -> none  [the longest x3 4.22 us: attend_block(): jnp.einsum('qk,kd->qd', dscore, all_keys, preferred_element_type=jnp.floa...]
    all_to_all x5 -> x0, waiting for transfers between devices: 13.1 us -> none  [the longest x1 5.76 us: per_device(): lax.all_to_all(img_grad, 'seq', split_axis=1, concat_axis=0, tiled=True)]
  transfers between devices with their start and end apart: 9 -> 0, of which waited for: 7 -> 0; matrix products, arithmetic and copies ran while one was open for 5% -> 0% of each run, Pallas kernels for 0% -> 0%
where the time goes in v1:
time: 60 us; the launch traced here: 59.7 us
  Pallas kernels  50.3 us (84%)
  local copies, waits for them, and re-layouts  8.72 us (15%)
  between operations  0.66 us (1%)
    pallas_call x1, Pallas kernels, per_device(): pl.pallas_call(body, out_shape=[jax.ShapeDtypeStruct((16, 2048), F32)] *...  50.3 us
    unnamed x16, local copies, waits for them, and re-layouts  8.72 us

profile of v1, /device:TPU:1, one launch (start us, length us, event | category | flops | bytes accessed | tf_op | source)
XLA Modules:
  0.0 59.7 jit_solution(14874905308859278864)
XLA Ops:
  0.6 0.0 copy-start
  0.6 1.6 %copy-done = bf16[512,2048]{1,0:T(8,128)(2,1)S(1)} copy-done((bf16[512,2048]{1,0:T(8,128)(2,1)S(1)}, bf16[512,2048]{1,0:T(8,128)(2,1)}, u32[]{:S(2)}) %copy-start) | copy-done | bytes 2097176
  2.2 0.0 copy-start.1
  2.2 0.8 %copy-done.1 = bf16[16,2048]{1,0:T(8,128)(2,1)S(1)} copy-done((bf16[16,2048]{1,0:T(8,128)(2,1)S(1)}, bf16[16,2048]{1,0:T(8,128)(2,1)}, u32[]{:S(2)}) %copy-start.1) | copy-done | bytes 65560
  3.1 0.0 copy-start.2
  3.1 0.8 %copy-done.2 = bf16[16,2048]{1,0:T(8,128)(2,1)S(1)} copy-done((bf16[16,2048]{1,0:T(8,128)(2,1)S(1)}, bf16[16,2048]{1,0:T(8,128)(2,1)}, u32[]{:S(2)}) %copy-start.2) | copy-done | bytes 65560
  3.9 0.0 copy-start.3
  3.9 0.8 %copy-done.3 = bf16[16,2048]{1,0:T(8,128)(2,1)S(1)} copy-done((bf16[16,2048]{1,0:T(8,128)(2,1)S(1)}, bf16[16,2048]{1,0:T(8,128)(2,1)}, u32[]{:S(2)}) %copy-start.3) | copy-done | bytes 65560
  4.7 0.0 copy-start.4
  4.7 0.8 %copy-done.4 = bf16[16,2048]{1,0:T(8,128)(2,1)S(1)} copy-done((bf16[16,2048]{1,0:T(8,128)(2,1)S(1)}, bf16[16,2048]{1,0:T(8,128)(2,1)}, u32[]{:S(2)}) %copy-start.4) | copy-done | bytes 65560
  5.6 50.3 %shard_map.127 = (f32[16,2048]{1,0:T(8,128)S(1)}, f32[16,2048]{1,0:T(8,128)S(1)}, f32[16,2048]{1,0:T(8,128)S(1)}, f32[32,128]{1,0:T(8,128)S(1)}, f32[32,128]{1,0:T(8,128)S(1)}, /*index=5*/f32[32,128]{1,0:T(8,128)S(1)}) custom-call(bf16[512,2048]{1,0:T(8,128)(2,1)S(1)} %copy-done, bf16[512,2048]{1,0:T(8,128)(2,1)} %tk.1, bf16[512,2048]{1,0:T(8,128)(2,1)} %tv.1, ...), custom_call_target="tpu_custom_call" | custom-call | flops 1700000000 | bytes 2000000 | tf_op jit(solution)/shard_map/pallas_call | solution.py:336
  55.9 0.7 %copy.20 = f32[16,2048]{1,0:T(8,128)} copy(f32[16,2048]{1,0:T(8,128)S(1)} %get-tuple-element.12) | data formatting | bytes 262144
  56.6 0.7 %copy.21 = f32[16,2048]{1,0:T(8,128)} copy(f32[16,2048]{1,0:T(8,128)S(1)} %get-tuple-element.13) | data formatting | bytes 262144
  57.2 0.7 %copy.22 = f32[16,2048]{1,0:T(8,128)} copy(f32[16,2048]{1,0:T(8,128)S(1)} %get-tuple-element.14) | data formatting | bytes 262144
  57.9 0.6 %copy.23 = f32[32,128]{1,0:T(8,128)} copy(f32[32,128]{1,0:T(8,128)S(1)} %get-tuple-element.15) | data formatting | bytes 32768
  58.5 0.6 %copy.24 = f32[32,128]{1,0:T(8,128)} copy(f32[32,128]{1,0:T(8,128)S(1)} %get-tuple-element.16) | data formatting | bytes 32768
  59.1 0.6 %copy.25 = f32[32,128]{1,0:T(8,128)} copy(f32[32,128]{1,0:T(8,128)S(1)} %get-tuple-element.17) | data formatting | bytes 32768
Async XLA Ops:
  0.6 1.6 %copy-start = (bf16[512,2048]{1,0:T(8,128)(2,1)S(1)}, bf16[512,2048]{1,0:T(8,128)(2,1)}, u32[]{:S(2)}) copy-start(bf16[512,2048]{1,0:T(8,128)(2,1)} %tq.1) | copy-start | bytes 6291460
  2.2 0.8 %copy-start.1 = (bf16[16,2048]{1,0:T(8,128)(2,1)S(1)}, bf16[16,2048]{1,0:T(8,128)(2,1)}, u32[]{:S(2)}) copy-start(bf16[16,2048]{1,0:T(8,128)(2,1)} %iq.1) | copy-start | bytes 196612
  3.1 0.8 %copy-start.2 = (bf16[16,2048]{1,0:T(8,128)(2,1)S(1)}, bf16[16,2048]{1,0:T(8,128)(2,1)}, u32[]{:S(2)}) copy-start(bf16[16,2048]{1,0:T(8,128)(2,1)} %ik.1) | copy-start | bytes 196612
  3.9 0.8 %copy-start.3 = (bf16[16,2048]{1,0:T(8,128)(2,1)S(1)}, bf16[16,2048]{1,0:T(8,128)(2,1)}, u32[]{:S(2)}) copy-start(bf16[16,2048]{1,0:T(8,128)(2,1)} %iv.1) | copy-start | bytes 196612
  4.7 0.8 %copy-start.4 = (bf16[16,2048]{1,0:T(8,128)(2,1)S(1)}, bf16[16,2048]{1,0:T(8,128)(2,1)}, u32[]{:S(2)}) copy-start(bf16[16,2048]{1,0:T(8,128)(2,1)} %ig.1) | copy-start | bytes 196612

commit v2 on v0

v2 whole, which is shorter than its diff:
```python
import jax
import jax.numpy as jnp
from jax import lax
from jax.experimental import pallas as pl
from jax.experimental.pallas import tpu as pltpu
from jax.sharding import PartitionSpec as P

HD = 128
LOG2E = 1.4426950408889634
SCALE = HD ** -0.5
UNIT = SCALE * LOG2E
BF = jnp.bfloat16
F32 = jnp.float32
MESH = pl.DeviceIdType.MESH

START = (0, 128, 384, 640, 896)
SIZE = (128, 256, 256, 256, 256)
ROWS = 1152


def nt(a, b):
    return lax.dot_general(a, b, (((1,), (1,)), ((), ())), preferred_element_type=F32)


def nn(a, b):
    return lax.dot_general(a, b, (((1,), (0,)), ((), ())), preferred_element_type=F32)


def body(
    tq, tk, tv, tg, iq, ik, iv, ig,
    fin, tfin,
    flat, stage, own, qg, kv, text,
    qall, kall, vall, gall, ktall,
    e_buf, dp_buf, pb_buf, ds_buf, mx, sm, dl, st, st_in,
    dkv_st, dkv_in, dkv_own, dkvt_st, dkvt_in, dkvt_own,
    dq_st, dq_in, dq_own, dqt_st, dqt_in, dq_text,
    out_st, tout,
    in_sem, text_sem,
    p1_s, p1_r, near_r, qg_s, qg_r, kv_s, kv_r, st_s, st_r,
    dkv_s, dkv_r, dkvt_s, dkvt_r, dq_s, dq_r, dqt_s, dqt_r,
    p4_s, p4_r, tx_s, tx_r,
):
    s = lax.axis_index("seq")
    m = lax.axis_index("mlp")
    z0, y, core = s // 8, (s // 2) % 4, s % 2
    x, zh = m // 4, m % 4

    def flip(j):
        zf = 1 - z0 if j & 2 else z0
        cf = 1 - core if j & 1 else core
        return zf * 8 + y * 2 + cf

    def turn(j):
        return z0 * 8 + ((y + j) % 4) * 2 + core

    def around(i, sign):
        dz, dx = i // 4, i % 4
        return ((x + sign * dx + 4) % 4) * 4 + (zh + sign * dz + 4) % 4

    far_first = (10, 9, 11, 8, 6, 14, 5, 13, 7, 15, 4, 12, 2, 1, 3)
    sends = []

    def send(src, dst, ss, rs, seq, mlp):
        c = pltpu.make_async_remote_copy(
            src, dst, ss, rs, device_id={"seq": seq, "mlp": mlp}, device_id_type=MESH)
        c.start()
        sends.append(c)

    def arrive(ref, sem):
        pltpu.make_async_copy(ref, ref, sem).wait()

    loads = []
    for n, ref in enumerate((iq, ig, ik, iv)):
        c = pltpu.make_async_copy(ref, flat.at[n], in_sem.at[n])
        c.start()
        loads.append(c)

    barrier = pltpu.get_barrier_semaphore()
    for i in far_first:
        pl.semaphore_signal(barrier, inc=1, device_id={"seq": s, "mlp": around(i, 1)}, device_id_type=MESH)

    @pl.when(s != m)
    def _():
        pl.semaphore_signal(barrier, inc=1, device_id={"seq": m, "mlp": s}, device_id_type=MESH)

    for j in (2, 3, 1):
        pl.semaphore_signal(barrier, inc=1, device_id={"seq": turn(j), "mlp": m}, device_id_type=MESH)
        pl.semaphore_signal(barrier, inc=1, device_id={"seq": flip(j), "mlp": m}, device_id_type=MESH)

    for n, c in enumerate(loads):
        c.wait()
        for h in range(16):
            stage[h, n] = flat[n, :, h * HD:(h + 1) * HD]

    @pl.when(s != m)
    def _():
        pl.semaphore_wait(barrier, 22)

    @pl.when(s == m)
    def _():
        pl.semaphore_wait(barrier, 21)

    for i in (1, 3, 2, 10, 9, 11, 8, 6, 14, 5, 13, 7, 15, 4, 12):
        dest = around(i, -1)
        send(stage.at[dest], own.at[i], p1_s.at[i], p1_r.at[i], s, dest)
    own[0] = stage[m]

    col = pl.ds(pl.multiple_of(m * HD, HD), HD)
    tloads = []
    for n, ref in enumerate((tq, tg, tk, tv)):
        for j in range(4):
            owner = (j // 2) * 8 + y * 2 + j % 2 if n < 2 else turn((4 - j) % 4)
            rows = pl.ds(pl.multiple_of(owner * 32, 32), 32)
            c = pltpu.make_async_copy(ref.at[rows, col], text.at[n, pl.ds(j * 32, 32)], text_sem.at[n, j])
            c.start()
            tloads.append(c)
    for c in tloads:
        c.wait()
    qall[0:128] = text[0]
    gall[0:128] = text[1]
    kall[0:128] = text[2]
    vall[0:128] = text[3]

    def copy(src, dst, ss, rs, seq):
        pltpu.make_async_remote_copy(
            src, dst, ss, rs, device_id={"seq": seq, "mlp": m}, device_id_type=MESH).start()

    def relay(g):
        part = pl.ds(4 * g, 4)
        arrive(qg.at[1, part], near_r.at[g])
        copy(qg.at[1, part], qg.at[2, part], qg_s.at[2], qg_r.at[2], flip(1))

    for n, i in enumerate((0, 1, 3, 2, 4, 12, 5, 13, 7, 15, 6, 14, 8, 9, 11, 10)):
        if i:
            arrive(own.at[i], p1_r.at[i])
        for j in (2, 1, 3):
            copy(own.at[i, pl.ds(2, 2)], kv.at[j - 1, i], kv_s.at[j - 1], kv_r.at[j - 1], turn(j))
        copy(own.at[i, pl.ds(0, 2)], qg.at[1, i], qg_s.at[1], near_r.at[i // 4], flip(2))
        copy(own.at[i, pl.ds(0, 2)], qg.at[0, i], qg_s.at[0], qg_r.at[0], flip(1))
        if n == 12:
            relay(0)

    def query_rows(qc):
        return pl.ds(START[qc], SIZE[qc])

    def width(qc):
        return 128 if qc == 0 else 256

    def key_rows(kc):
        return pl.ds(START[kc], SIZE[kc])

    def pass_one(kc, qc):
        kr, qr, n = key_rows(kc), query_rows(qc), pl.ds(0, width(qc))
        scores = nt(kall[kr], qall[qr])
        top = jnp.max(scores, axis=0, keepdims=True)
        e = jnp.exp2((scores - top) * UNIT)
        dp = nt(vall[kr], gall[qr])
        mx[qc, kc:kc + 1, n] = top
        sm[qc, kc:kc + 1, n] = jnp.sum(e, axis=0, keepdims=True)
        dl[qc, kc:kc + 1, n] = jnp.sum(e * dp, axis=0, keepdims=True)
        e_buf[qc, kr, n] = e
        dp_buf[qc, kr, n] = dp

    def take_keys(j):
        if j:
            arrive(kv.at[j - 1], kv_r.at[j - 1])
            k, v = kv[j - 1, :, 0], kv[j - 1, :, 1]
        else:
            k, v = own[:, 2], own[:, 3]
        r = key_rows(j + 1)
        kall[r] = k.reshape(256, HD)
        vall[r] = v.reshape(256, HD)

    def take_queries(j):
        if j:
            if j != 2:
                arrive(qg.at[j - 1], qg_r.at[j - 1])
            q, g_ = qg[j - 1, :, 0], qg[j - 1, :, 1]
        else:
            q, g_ = own[:, 0], own[:, 1]
        r = query_rows(j + 1)
        qall[r] = q.reshape(256, HD)
        gall[r] = g_.reshape(256, HD)

    take_queries(0)
    take_keys(0)
    for kc in (0, 1):
        pass_one(kc, 0)
        pass_one(kc, 1)
    take_queries(1)
    for kc in (0, 1):
        pass_one(kc, 2)
    relay(1)
    relay(3)
    relay(2)
    take_queries(2)
    for kc in (0, 1):
        pass_one(kc, 3)
    for j in (1, 3):
        take_keys(j)
        pass_one(j + 1, 0)
        for i in range(3):
            pass_one(j + 1, i + 1)
    take_queries(3)
    for kc in (0, 1, 2, 4):
        pass_one(kc, 4)
    take_keys(2)

    for qc in range(5):
        pass_one(3, qc)
        n = pl.ds(0, width(qc))
        top = jnp.max(mx[qc, 0:5, n], axis=0, keepdims=True)
        w = jnp.exp2((mx[qc, 0:5, n] - top) * UNIT)
        total = jnp.sum(w * sm[qc, 0:5, n], axis=0, keepdims=True)
        dsum = jnp.sum(w * dl[qc, 0:5, n], axis=0, keepdims=True)
        for i, row in enumerate((top, total, dsum)):
            for half in range(1 if qc == 0 else 2):
                b = 2 * qc - 1 + half if qc else 0
                st[i * 9 + b:i * 9 + b + 1] = row[:, half * 128:(half + 1) * 128]
    for j in (2, 3, 1):
        send(st, st_in.at[j - 1], st_s.at[j - 1], st_r.at[j - 1], flip(j), m)
    ktall[...] = kall[...].T
    for j in (1, 2, 3):
        arrive(st_in.at[j - 1], st_r.at[j - 1])

    def theirs(j, first):
        rows = [0] + [1 + 2 * (r ^ j) + half for r in range(4) for half in range(2)]
        return jnp.concatenate([st_in[j - 1, first + b:first + b + 1] for b in rows], axis=0)

    tops, sums, dsums = ([st[n:n + 9]] + [theirs(j, n) for j in (1, 2, 3)] for n in (0, 9, 18))
    gtop = jnp.maximum(jnp.maximum(tops[0], tops[1]), jnp.maximum(tops[2], tops[3]))
    ws = [jnp.exp2((t - gtop) * UNIT) for t in tops]
    gsum = sum(w * t for w, t in zip(ws, sums))
    gd = sum(w * t for w, t in zip(ws, dsums))
    inv = 1.0 / gsum

    delta = gd * inv

    def as_row(a, qc):
        if qc == 0:
            return a[0:1]
        return jnp.concatenate([a[2 * qc - 1:2 * qc], a[2 * qc:2 * qc + 1]], axis=1)

    for qc in range(5):
        n = pl.ds(0, width(qc))
        mx[qc, 0:5, n] = jnp.exp2((mx[qc, 0:5, n] - as_row(gtop, qc)) * UNIT) * as_row(inv, qc)
        dl[qc, 0:1, n] = as_row(delta, qc)

    def probs(kc, qc):
        kr, qr, n = key_rows(kc), query_rows(qc), pl.ds(0, width(qc))
        p = e_buf[qc, kr, n] * mx[qc, kc:kc + 1, n]
        pb_buf[kr, qr] = p.astype(BF)
        ds_buf[kr, qr] = (p * (dp_buf[qc, kr, n] - dl[qc, 0:1, n])).astype(BF)

    def value_grad(kc):
        return nn(pb_buf[key_rows(kc)], gall[...])

    def key_grad(kc):
        return nn(ds_buf[key_rows(kc)], qall[...]) * SCALE

    def query_grad(qc):
        return (nn(ktall[...], ds_buf[:, query_rows(qc)]) * SCALE).T

    def text_part(j):
        peer = flip(j)
        return pl.ds(pl.multiple_of((peer // 8 * 2 + peer % 2) * 32, 32), 32)

    def group(g):
        return pl.ds(64 * g, 64)

    FAR = (2, 1, 3, 0)

    def keys_out(kc):
        j = kc - 1
        dv, dk = value_grad(kc).astype(BF), key_grad(kc).astype(BF)
        for g in FAR:
            dkv_st[j - 1, g, 0] = dk[64 * g:64 * g + 64]
            dkv_st[j - 1, g, 1] = dv[64 * g:64 * g + 64]
            send(dkv_st.at[j - 1, g], dkv_in.at[j - 1, g], dkv_s.at[j - 1, g], dkv_r.at[j - 1, g], turn(4 - j), m)

    for qc in range(5):
        probs(0, qc)
    dk, dv = key_grad(0), value_grad(0)
    dkvt_own[0] = dk[0:32]
    dkvt_own[1] = dv[0:32]
    for j in (2, 1, 3):
        part = slice(j * 32, j * 32 + 32)
        dkvt_st[j - 1, 0] = dk[part].astype(BF)
        dkvt_st[j - 1, 1] = dv[part].astype(BF)
        send(dkvt_st.at[j - 1], dkvt_in.at[j - 1], dkvt_s.at[j - 1], dkvt_r.at[j - 1], turn(4 - j), m)
    for qc in range(5):
        probs(3, qc)
    keys_out(3)
    for kc in (2, 4, 1):
        probs(kc, 0)
    dq_text[...] = query_grad(0)
    for j in (2, 3, 1):
        dqt_st[j - 1] = dq_text[text_part(j)].astype(BF)
        send(dqt_st.at[j - 1], dqt_in.at[j - 1], dqt_s.at[j - 1], dqt_r.at[j - 1], flip(j), m)
    for kc in (2, 4):
        for qc in range(1, 5):
            probs(kc, qc)
        keys_out(kc)
    for qc in range(1, 5):
        probs(1, qc)

    for j in (2, 3, 1, 0):
        dq = query_grad(j + 1)
        if j == 0:
            dq_own[...] = dq
            continue
        dq_st[j - 1] = dq.astype(BF)
        for g in FAR:
            rows = group(g)
            send(dq_st.at[j - 1, rows], dq_in.at[j - 1, rows], dq_s.at[j - 1, g], dq_r.at[j - 1, g], flip(j), m)

    own_v = value_grad(1)
    own_k = key_grad(1)
    dkv_own[0] = own_k
    dkv_own[1] = own_v

    for j in range(3):
        arrive(dqt_in.at[j], dqt_r.at[j])
        arrive(dkvt_in.at[j], dkvt_r.at[j])

    def plus(own_term, terms):
        for t in terms:
            own_term = own_term + t.astype(F32)
        return own_term

    tout[0] = plus(dq_text[text_part(0)], [dqt_in[j] for j in range(3)]).astype(BF)
    tout[1] = plus(dkvt_own[0], [dkvt_in[j, 0] for j in range(3)]).astype(BF)
    tout[2] = plus(dkvt_own[1], [dkvt_in[j, 1] for j in range(3)]).astype(BF)
    tcopy = pltpu.make_async_remote_copy(
        tout, tfin, tx_s, tx_r, device_id={"seq": m, "mlp": s}, device_id_type=MESH)

    @pl.when(s != m)
    def _():
        tcopy.start()

    @pl.when(s == m)
    def _():
        tfin[...] = tout[...]

    for g in FAR:
        slots = pl.ds(4 * g, 4)
        for j in range(3):
            arrive(dkv_in.at[j, g], dkv_r.at[j, g])
        for n in (0, 1):
            total = plus(dkv_own[n, group(g)], [dkv_in[j, g, n] for j in range(3)])
            out_st[slots, n + 1] = total.astype(BF).reshape(4, 16, HD)
        for j in range(3):
            arrive(dq_in.at[j, group(g)], dq_r.at[j, g])
        total = plus(dq_own[group(g)], [dq_in[j, group(g)] for j in range(3)])
        out_st[slots, 0] = total.astype(BF).reshape(4, 16, HD)
        for i in (4 * g + 2, 4 * g + 1, 4 * g + 3, 4 * g):
            if i:
                send(out_st.at[i], fin.at[m], p4_s.at[i], p4_r.at[i], s, around(i, 1))
    fin[m] = out_st[0]

    for j in range(3):
        arrive(kv.at[j], kv_s.at[j])
        arrive(qg.at[j], qg_s.at[j])
    for c in sends:
        c.wait_send()
    for i in far_first:
        arrive(fin.at[around(i, -1)], p4_r.at[i])

    @pl.when(s != m)
    def _():
        tcopy.wait()


def widen(fin, tfin, oq, ok, ov, otq, otk, otv):
    for n, out in enumerate((oq, ok, ov)):
        for h in range(16):
            out[:, h * HD:(h + 1) * HD] = fin[h, n].astype(F32)
    for n, out in enumerate((otq, otk, otv)):
        out[...] = tfin[n].astype(F32)


def per_device(*args):
    hbm = pl.BlockSpec(memory_space=pltpu.HBM)
    vmem = pl.BlockSpec(memory_space=pltpu.VMEM)
    sem = pltpu.SemaphoreType.DMA
    V = pltpu.VMEM
    landed = pl.pallas_call(
        body,
        out_shape=[pltpu.VMEM((16, 3, 16, HD), BF), pltpu.VMEM((3, 32, HD), BF)],
        in_specs=[hbm] * 8,
        out_specs=[vmem] * 2,
        scratch_shapes=[
            V((4, 16, 2048), BF), V((16, 4, 16, HD), BF), V((16, 4, 16, HD), BF),
            V((3, 16, 2, 16, HD), BF), V((3, 16, 2, 16, HD), BF), V((4, 128, HD), BF),
            V((ROWS, HD), BF), V((ROWS, HD), BF), V((ROWS, HD), BF), V((ROWS, HD), BF), V((HD, ROWS), BF),
            V((5, ROWS, 256), F32), V((5, ROWS, 256), F32), V((ROWS, ROWS), BF), V((ROWS, ROWS), BF),
            V((5, 8, 256), F32), V((5, 8, 256), F32), V((5, 8, 256), F32), V((32, HD), F32), V((3, 32, HD), F32),
            V((3, 4, 2, 64, HD), BF), V((3, 4, 2, 64, HD), BF), V((2, 256, HD), F32),
            V((3, 2, 32, HD), BF), V((3, 2, 32, HD), BF), V((2, 32, HD), F32),
            V((3, 256, HD), BF), V((3, 256, HD), BF), V((256, HD), F32),
            V((3, 32, HD), BF), V((3, 32, HD), BF), V((HD, HD), F32),
            V((16, 3, 16, HD), BF), V((3, 32, HD), BF),
            sem((4,)), sem((4, 4)),
            sem((16,)), sem((16,)), sem((4,)), sem((3,)), sem((3,)), sem((3,)), sem((3,)), sem((3,)), sem((3,)),
            sem((3, 4)), sem((3, 4)), sem((3,)), sem((3,)), sem((3, 4)), sem((3, 4)), sem((3,)), sem((3,)),
            sem((16,)), sem((16,)), sem, sem,
        ],
        compiler_params=pltpu.CompilerParams(
            collective_id=0, has_side_effects=True, vmem_limit_bytes=48 * 1024 * 1024),
        cost_estimate=pl.CostEstimate(flops=1_700_000_000, bytes_accessed=2_000_000, transcendentals=1_300_000),
    )(*[pltpu.with_memory_space_constraint(a, pltpu.HBM) for a in args])
    return pl.pallas_call(
        widen,
        out_shape=[jax.ShapeDtypeStruct((16, 2048), F32)] * 3 + [jax.ShapeDtypeStruct((32, HD), F32)] * 3,
        in_specs=[vmem] * 2,
        out_specs=[vmem] * 6,
        compiler_params=pltpu.CompilerParams(vmem_limit_bytes=4 * 1024 * 1024),
    )(*landed)


def solution(mesh):
    tokens = P(("seq", "mlp"), None)
    return jax.shard_map(
        per_device,
        mesh=mesh,
        in_specs=(P(), P(), P(), P(), tokens, tokens, tokens, tokens),
        out_specs=(tokens, tokens, tokens, P("mlp", "seq"), P("mlp", "seq"), P("mlp", "seq")),
        check_vma=False,
    )
```

time: 428 us -> 48.9 us (0.11)
  waiting for transfers between devices: 312 us -> 0 us
  Pallas kernels: 0 us -> 48 us
  starting transfers between devices: 35.6 us -> 0 us
  blocking collectives: 22.5 us -> 0 us
  local copies, waits for them, and re-layouts: 19.5 us -> 0 us
  matrix products: 16.6 us -> 0 us
  between operations: 14.1 us -> 0.64 us
  other arithmetic: 6.79 us -> 0 us
    psum x1 -> x0, waiting for transfers between devices: 149 us -> none  [per_device(): summed = lax.psum(key_terms[:text_total], 'mlp')]
    reduce_scatter x1 -> x0, waiting for transfers between devices: 80 us -> none  [per_device(): lax.psum_scatter(scatter_terms, 'mlp', scatter_dimension=0, tiled=True)]
    all_gather x2 -> x0, waiting for transfers between devices: 70.1 us -> none  [the longest x1 49 us: per_device(): lax.all_gather(local_v, 'mlp', axis=0, tiled=True)]
    pallas_call x0 -> x2, Pallas kernels: none -> 48 us  [the longest x1 47.3 us: per_device(): pl.pallas_call(body, out_shape=[pltpu.VMEM((16, 3, 16, HD), BF), pltpu.VM...]
    all_to_all x5 -> x0, starting transfers between devices: 35.5 us -> none  [the longest x1 15.8 us: per_device(): lax.all_to_all(owned[:, head_width:], 'seq', split_axis=0, concat_axis=1,...]
    all_to_all x2 -> x0, blocking collectives: 22.5 us -> none  [the longest x1 13.1 us: per_device(): lax.all_to_all(img_k, 'seq', split_axis=1, concat_axis=0, tiled=True)]
    dot_general x15 -> x0, matrix products: 16.6 us -> none  [the longest x3 4.22 us: attend_block(): jnp.einsum('qk,kd->qd', dscore, all_keys, preferred_element_type=jnp.floa...]
    all_to_all x5 -> x0, waiting for transfers between devices: 13.1 us -> none  [the longest x1 5.76 us: per_device(): lax.all_to_all(img_grad, 'seq', split_axis=1, concat_axis=0, tiled=True)]
  transfers between devices with their start and end apart: 9 -> 0, of which waited for: 7 -> 0; matrix products, arithmetic and copies ran while one was open for 5% -> 0% of each run, Pallas kernels for 0% -> 0%
where the time goes in v2:
time: 48.9 us; the launch traced here: 48.7 us
  Pallas kernels  48 us (98%)
  between operations  0.64 us (1%)
    pallas_call x1, Pallas kernels, per_device(): pl.pallas_call(body, out_shape=[pltpu.VMEM((16, 3, 16, HD), BF), pltpu.VM...  47.3 us

profile of v2, /device:TPU:1, one launch (start us, length us, event | category | flops | bytes accessed | tf_op | source)
XLA Modules:
  0.0 48.7 jit_solution(14083159082488782330)
XLA Ops:
  0.6 47.3 %shard_map.127 = (bf16[16,3,16,128]{3,2,1,0:T(8,128)(2,1)S(1)}, bf16[3,32,128]{2,1,0:T(8,128)(2,1)S(1)}) custom-call(bf16[512,2048]{1,0:T(8,128)(2,1)} %tq.1, bf16[512,2048]{1,0:T(8,128)(2,1)} %tk.1, bf16[512,2048]{1,0:T(8,128)(2,1)} %tv.1, bf16[512,2048]{1,0:T(8,128)(2,1)} %tg.1, bf16[16,2048]{1,0:T(8,128)(2,1)} %iq.1, bf16[16,2048]{1,0:T(8,128)(2,1)} %ik.1, ...), custom_call_target="tpu_custom_call" | custom-call | flops 1700000000 | bytes 2000000 | tf_op jit(solution)/shard_map/pallas_call | solution.py:387
  47.9 0.8 %shard_map.128 = (f32[16,2048]{1,0:T(8,128)}, f32[16,2048]{1,0:T(8,128)}, f32[16,2048]{1,0:T(8,128)}, f32[32,128]{1,0:T(8,128)}, f32[32,128]{1,0:T(8,128)}, /*index=5*/f32[32,128]{1,0:T(8,128)}) custom-call(bf16[16,3,16,128]{3,2,1,0:T(8,128)(2,1)S(1)} %get-tuple-element.8.fin, bf16[3,32,128]{2,1,0:T(8,128)(2,1)S(1)} %get-tuple-element.9.tfin), custom_call_target="tpu_custom_call" | custom-call | tf_op jit(solution)/shard_map/pallas_call | solution.py:412

commit v3 on v2

v3 whole, which is shorter than its diff:
```python
import jax
import jax.numpy as jnp
from jax import lax
from jax.experimental import pallas as pl
from jax.experimental.pallas import tpu as pltpu
from jax.sharding import PartitionSpec as P

HD = 128
LOG2E = 1.4426950408889634
SCALE = HD ** -0.5
UNIT = SCALE * LOG2E
BF = jnp.bfloat16
F32 = jnp.float32
MESH = pl.DeviceIdType.MESH

SLOTS = ((0, 0), (0, 1), (1, 0), (7, 0), (1, 1), (7, 1), (2, 0), (6, 0),
         (2, 1), (6, 1), (3, 0), (5, 0), (3, 1), (5, 1), (4, 0), (4, 1))

START = (0, 128, 384, 640, 896)
SIZE = (128, 256, 256, 256, 256)
ROWS = 1152


def nt(a, b):
    return lax.dot_general(a, b, (((1,), (1,)), ((), ())), preferred_element_type=F32)


def nn(a, b):
    return lax.dot_general(a, b, (((1,), (0,)), ((), ())), preferred_element_type=F32)


def body(
    tq, tk, tv, tg, iq, ik, iv, ig,
    fin, tfin,
    flat, stage, own, qg, kv, text,
    qall, kall, vall, gall, ktall,
    e_buf, dp_buf, pb_buf, ds_buf, mx, sm, dl, st, st_in,
    dkv_st, dkv_in, dkv_own, dkvt_st, dkvt_in, dkvt_own,
    dq_st, dq_in, dq_own, dqt_st, dqt_in, dq_text,
    out_st, tout,
    in_sem, text_sem,
    p1_s, p1_r, qg_s, qg_r, ql, kv_s, kv_r, st_s, st_r,
    dkv_s, dkv_r, dkvt_s, dkvt_r, dq_s, dq_r, dqt_s, dqt_r,
    p4_s, p4_r, tx_s, tx_r,
):
    seq = lax.axis_index("seq")
    mlp = lax.axis_index("mlp")
    z0, y, core = seq // 8, (seq // 2) % 4, seq % 2
    x, zh = mlp // 4, mlp % 4
    z = zh * 2 + z0

    head = z0 * 8 + zh * 2 + core
    u = x * (1 - core) + y * core
    v = y * (1 - core) + x * core

    def along(jx, jy):
        return {"seq": z0 * 8 + ((y + jy) % 4) * 2 + core, "mlp": ((x + jx) % 4) * 4 + zh}

    def shift(j):
        return along(j * (1 - core), j * core)

    def turn(j):
        return along(j * core, j * (1 - core))

    def block(a, b):
        return a * (4 - 3 * core) + b * (1 + 3 * core)

    def around(i, sign):
        dz, dc = SLOTS[i]
        there = (z + sign * dz + 8) % 8
        other = 1 - core if dc else core
        return there % 2, there // 2, other

    def column(i, sign):
        zo, zi, other = around(i, sign)
        return {"seq": zo * 8 + y * 2 + other, "mlp": x * 4 + zi}

    def head_of(i, sign):
        zo, zi, other = around(i, sign)
        return zo * 8 + zi * 2 + other

    partner = {"seq": z0 * 8 + zh * 2 + core, "mlp": x * 4 + y}
    sends = []

    def send(src, dst, ss, rs, to):
        c = pltpu.make_async_remote_copy(src, dst, ss, rs, device_id=to, device_id_type=MESH)
        c.start()
        sends.append(c)

    def arrive(ref, sem):
        pltpu.make_async_copy(ref, ref, sem).wait()

    loads = []
    for n, ref in enumerate((iq, ig, ik, iv)):
        c = pltpu.make_async_copy(ref, flat.at[n], in_sem.at[n])
        c.start()
        loads.append(c)

    barrier = pltpu.get_barrier_semaphore()
    def greet(to):
        pl.semaphore_signal(barrier, inc=1, device_id=to, device_id_type=MESH)

    for i in range(15, 0, -1):
        greet(column(i, 1))

    @pl.when(y != zh)
    def _():
        greet(partner)

    for j in (2, 3, 1):
        greet(turn(j))
        greet(shift(j))

    for n, c in enumerate(loads):
        c.wait()
        for h in range(16):
            stage[h, n] = flat[n, :, h * HD:(h + 1) * HD]

    @pl.when(y != zh)
    def _():
        pl.semaphore_wait(barrier, 22)

    @pl.when(y == zh)
    def _():
        pl.semaphore_wait(barrier, 21)

    for i in range(1, 16):
        send(stage.at[head_of(i, -1)], own.at[i], p1_s.at[i], p1_r.at[i], column(i, -1))
    own[0] = stage[head]

    col = pl.ds(pl.multiple_of(head * HD, HD), HD)
    tloads = []
    for n, ref in enumerate((tq, tg, tk, tv)):
        for j in range(4):
            owner = block(j, v) if n < 2 else block(u, (v + 4 - j) % 4)
            rows = pl.ds(pl.multiple_of(owner * 32, 32), 32)
            c = pltpu.make_async_copy(ref.at[rows, col], text.at[n, pl.ds(j * 32, 32)], text_sem.at[n, j])
            c.start()
            tloads.append(c)
    for c in tloads:
        c.wait()
    qall[0:128] = text[0]
    gall[0:128] = text[1]
    kall[0:128] = text[2]
    vall[0:128] = text[3]

    for i in range(16):
        if i:
            arrive(own.at[i], p1_r.at[i])
        g = i // 4
        for j in (2, 1, 3):
            pltpu.make_async_remote_copy(
                own.at[i, pl.ds(2, 2)], kv.at[j - 1, i], kv_s.at[j - 1], kv_r.at[j - 1, g],
                device_id=turn(j), device_id_type=MESH).start()
            pltpu.make_async_remote_copy(
                own.at[i, pl.ds(0, 2)], qg.at[u, i], qg_s.at[j - 1], qg_r.at[u, g],
                device_id=shift(j), device_id_type=MESH).start()
        pltpu.make_async_copy(own.at[i, pl.ds(0, 2)], qg.at[u, i], ql.at[g]).start()

    def query_rows(qc):
        return pl.ds(START[qc], SIZE[qc])

    def width(qc):
        return 128 if qc == 0 else 256

    def key_rows(kc):
        return pl.ds(START[kc], SIZE[kc])

    def pass_one(kc, qc):
        kr, qr, n = key_rows(kc), query_rows(qc), pl.ds(0, width(qc))
        scores = nt(kall[kr], qall[qr])
        top = jnp.max(scores, axis=0, keepdims=True)
        e = jnp.exp2((scores - top) * UNIT)
        dp = nt(vall[kr], gall[qr])
        mx[qc, kc:kc + 1, n] = top
        sm[qc, kc:kc + 1, n] = jnp.sum(e, axis=0, keepdims=True)
        dl[qc, kc:kc + 1, n] = jnp.sum(e * dp, axis=0, keepdims=True)
        e_buf[qc, kr, n] = e
        dp_buf[qc, kr, n] = dp

    def take(g):
        slots = pl.ds(4 * g, 4)
        for j in range(1, 4):
            arrive(kv.at[j - 1, slots], kv_r.at[j - 1, g])
            a = (u + 4 - j) % 4
            arrive(qg.at[a, slots], qg_r.at[a, g])
        arrive(qg.at[u, slots], ql.at[g])
        for b in range(4):
            r = pl.ds(START[g + 1] + 64 * b, 64)
            k, val = (kv[b - 1, slots, 0], kv[b - 1, slots, 1]) if b else (own[slots, 2], own[slots, 3])
            kall[r] = k.reshape(64, HD)
            vall[r] = val.reshape(64, HD)
            qall[r] = qg[b, slots, 0].reshape(64, HD)
            gall[r] = qg[b, slots, 1].reshape(64, HD)

    pass_one(0, 0)
    for g in range(4):
        take(g)
        for c in range(g + 1):
            pass_one(g + 1, c)
            pass_one(c, g + 1)
        if g < 3:
            pass_one(g + 1, g + 1)

    for qc in range(5):
        if qc == 4:
            pass_one(4, 4)
        n = pl.ds(0, width(qc))
        top = jnp.max(mx[qc, 0:5, n], axis=0, keepdims=True)
        w = jnp.exp2((mx[qc, 0:5, n] - top) * UNIT)
        total = jnp.sum(w * sm[qc, 0:5, n], axis=0, keepdims=True)
        dsum = jnp.sum(w * dl[qc, 0:5, n], axis=0, keepdims=True)
        for i, row in enumerate((top, total, dsum)):
            for half in range(1 if qc == 0 else 2):
                b = 2 * qc - 1 + half if qc else 0
                st[i * 9 + b:i * 9 + b + 1] = row[:, half * 128:(half + 1) * 128]
    for j in (2, 3, 1):
        send(st, st_in.at[j - 1], st_s.at[j - 1], st_r.at[j - 1], shift(j))
    ktall[...] = kall[...].T
    for j in (1, 2, 3):
        arrive(st_in.at[j - 1], st_r.at[j - 1])

    tops, sums, dsums = ([st[n:n + 9]] + [st_in[j, n:n + 9] for j in range(3)] for n in (0, 9, 18))
    gtop = jnp.maximum(jnp.maximum(tops[0], tops[1]), jnp.maximum(tops[2], tops[3]))
    ws = [jnp.exp2((t - gtop) * UNIT) for t in tops]
    gsum = sum(w * t for w, t in zip(ws, sums))
    gd = sum(w * t for w, t in zip(ws, dsums))
    inv = 1.0 / gsum

    delta = gd * inv

    def as_row(a, qc):
        if qc == 0:
            return a[0:1]
        return jnp.concatenate([a[2 * qc - 1:2 * qc], a[2 * qc:2 * qc + 1]], axis=1)

    for qc in range(5):
        n = pl.ds(0, width(qc))
        mx[qc, 0:5, n] = jnp.exp2((mx[qc, 0:5, n] - as_row(gtop, qc)) * UNIT) * as_row(inv, qc)
        dl[qc, 0:1, n] = as_row(delta, qc)

    def probs(kc, qc):
        kr, qr, n = key_rows(kc), query_rows(qc), pl.ds(0, width(qc))
        p = e_buf[qc, kr, n] * mx[qc, kc:kc + 1, n]
        pb_buf[kr, qr] = p.astype(BF)
        ds_buf[kr, qr] = (p * (dp_buf[qc, kr, n] - dl[qc, 0:1, n])).astype(BF)

    def value_grad(kc):
        return nn(pb_buf[key_rows(kc)], gall[...])

    def key_grad(kc):
        return nn(ds_buf[key_rows(kc)], qall[...]) * SCALE

    def query_grad(qc):
        return (nn(ktall[...], ds_buf[:, query_rows(qc)]) * SCALE).T

    def text_part(j):
        return pl.ds(pl.multiple_of(((u + 4 - j) % 4) * 32, 32), 32)

    FAR = (3, 2, 1, 0)

    def keys_out(g):
        dk, dv = key_grad(g + 1), value_grad(g + 1)
        dkv_own[g, 0] = dk[0:64]
        dkv_own[g, 1] = dv[0:64]
        for j in (2, 1, 3):
            dkv_st[j - 1, g, 0] = dk[64 * j:64 * j + 64].astype(BF)
            dkv_st[j - 1, g, 1] = dv[64 * j:64 * j + 64].astype(BF)
            send(dkv_st.at[j - 1, g], dkv_in.at[j - 1, g], dkv_s.at[j - 1, g], dkv_r.at[j - 1, g], turn(4 - j))

    def queries_out(g):
        dq = query_grad(g + 1).reshape(4, 64, HD)
        dq_own[g] = dq
        dq_st[g] = dq.astype(BF)
        for j in (2, 1, 3):
            send(dq_st.at[g, (u + 4 - j) % 4], dq_in.at[j - 1, g], dq_s.at[j - 1, g], dq_r.at[j - 1, g], shift(4 - j))

    for g in (3, 2):
        for qc in range(5):
            probs(g + 1, qc)
        keys_out(g)
    for qc in range(5):
        probs(0, qc)
    dk, dv = key_grad(0), value_grad(0)
    dkvt_own[0] = dk[0:32]
    dkvt_own[1] = dv[0:32]
    for j in (2, 1, 3):
        part = slice(j * 32, j * 32 + 32)
        dkvt_st[j - 1, 0] = dk[part].astype(BF)
        dkvt_st[j - 1, 1] = dv[part].astype(BF)
        send(dkvt_st.at[j - 1], dkvt_in.at[j - 1], dkvt_s.at[j - 1], dkvt_r.at[j - 1], turn(4 - j))
    for kc in (2, 1):
        probs(kc, 0)
    dq_text[...] = query_grad(0)
    for j in (2, 1, 3):
        dqt_st[j - 1] = dq_text[text_part(j)].astype(BF)
        send(dqt_st.at[j - 1], dqt_in.at[j - 1], dqt_s.at[j - 1], dqt_r.at[j - 1], shift(4 - j))
    for g in (1, 0):
        for qc in range(1, 5):
            probs(g + 1, qc)
        keys_out(g)
    for g in FAR:
        queries_out(g)

    for j in range(3):
        arrive(dqt_in.at[j], dqt_r.at[j])
        arrive(dkvt_in.at[j], dkvt_r.at[j])

    def plus(own_term, terms):
        for t in terms:
            own_term = own_term + t.astype(F32)
        return own_term

    tout[0] = plus(dq_text[text_part(0)], [dqt_in[j] for j in range(3)]).astype(BF)
    tout[1] = plus(dkvt_own[0], [dkvt_in[j, 0] for j in range(3)]).astype(BF)
    tout[2] = plus(dkvt_own[1], [dkvt_in[j, 1] for j in range(3)]).astype(BF)
    tcopy = pltpu.make_async_remote_copy(
        tout, tfin, tx_s, tx_r, device_id=partner, device_id_type=MESH)

    @pl.when(y != zh)
    def _():
        tcopy.start()

    @pl.when(y == zh)
    def _():
        tfin[...] = tout[...]

    for g in FAR:
        slots = pl.ds(4 * g, 4)
        for j in range(3):
            arrive(dkv_in.at[j, g], dkv_r.at[j, g])
        for n in (0, 1):
            total = plus(dkv_own[g, n], [dkv_in[j, g, n] for j in range(3)])
            out_st[slots, n + 1] = total.astype(BF).reshape(4, 16, HD)
        for j in range(3):
            arrive(dq_in.at[j, g], dq_r.at[j, g])
        total = plus(dq_own[g, u], [dq_in[j, g] for j in range(3)])
        out_st[slots, 0] = total.astype(BF).reshape(4, 16, HD)
        for i in range(4 * g, 4 * g + 4):
            if i:
                send(out_st.at[i], fin.at[head], p4_s.at[i], p4_r.at[i], column(i, 1))
    fin[head] = out_st[0]

    for j in range(3):
        arrive(kv.at[j], kv_s.at[j])
        arrive(kv.at[j], qg_s.at[j])
    for c in sends:
        c.wait_send()
    for i in range(15, 0, -1):
        arrive(fin.at[head_of(i, -1)], p4_r.at[i])

    @pl.when(y != zh)
    def _():
        tcopy.wait()


def widen(fin, tfin, oq, ok, ov, otq, otk, otv):
    for n, out in enumerate((oq, ok, ov)):
        for h in range(16):
            out[:, h * HD:(h + 1) * HD] = fin[h, n].astype(F32)
    for n, out in enumerate((otq, otk, otv)):
        out[...] = tfin[n].astype(F32)


def per_device(*args):
    hbm = pl.BlockSpec(memory_space=pltpu.HBM)
    vmem = pl.BlockSpec(memory_space=pltpu.VMEM)
    sem = pltpu.SemaphoreType.DMA
    V = pltpu.VMEM
    landed = pl.pallas_call(
        body,
        out_shape=[pltpu.VMEM((16, 3, 16, HD), BF), pltpu.VMEM((3, 32, HD), BF)],
        in_specs=[hbm] * 8,
        out_specs=[vmem] * 2,
        scratch_shapes=[
            V((4, 16, 2048), BF), V((16, 4, 16, HD), BF), V((16, 4, 16, HD), BF),
            V((4, 16, 2, 16, HD), BF), V((3, 16, 2, 16, HD), BF), V((4, 128, HD), BF),
            V((ROWS, HD), BF), V((ROWS, HD), BF), V((ROWS, HD), BF), V((ROWS, HD), BF), V((HD, ROWS), BF),
            V((5, ROWS, 256), F32), V((5, ROWS, 256), F32), V((ROWS, ROWS), BF), V((ROWS, ROWS), BF),
            V((5, 8, 256), F32), V((5, 8, 256), F32), V((5, 8, 256), F32), V((32, HD), F32), V((3, 32, HD), F32),
            V((3, 4, 2, 64, HD), BF), V((3, 4, 2, 64, HD), BF), V((4, 2, 64, HD), F32),
            V((3, 2, 32, HD), BF), V((3, 2, 32, HD), BF), V((2, 32, HD), F32),
            V((4, 4, 64, HD), BF), V((3, 4, 64, HD), BF), V((4, 4, 64, HD), F32),
            V((3, 32, HD), BF), V((3, 32, HD), BF), V((HD, HD), F32),
            V((16, 3, 16, HD), BF), V((3, 32, HD), BF),
            sem((4,)), sem((4, 4)),
            sem((16,)), sem((16,)), sem((3,)), sem((4, 4)), sem((4,)), sem((3,)), sem((3, 4)), sem((3,)), sem((3,)),
            sem((3, 4)), sem((3, 4)), sem((3,)), sem((3,)), sem((3, 4)), sem((3, 4)), sem((3,)), sem((3,)),
            sem((16,)), sem((16,)), sem, sem,
        ],
        compiler_params=pltpu.CompilerParams(
            collective_id=0, has_side_effects=True, vmem_limit_bytes=48 * 1024 * 1024),
        cost_estimate=pl.CostEstimate(flops=1_700_000_000, bytes_accessed=2_000_000, transcendentals=1_300_000),
    )(*[pltpu.with_memory_space_constraint(a, pltpu.HBM) for a in args])
    return pl.pallas_call(
        widen,
        out_shape=[jax.ShapeDtypeStruct((16, 2048), F32)] * 3 + [jax.ShapeDtypeStruct((32, HD), F32)] * 3,
        in_specs=[vmem] * 2,
        out_specs=[vmem] * 6,
        compiler_params=pltpu.CompilerParams(vmem_limit_bytes=4 * 1024 * 1024),
    )(*landed)


def solution(mesh):
    tokens = P(("seq", "mlp"), None)
    return jax.shard_map(
        per_device,
        mesh=mesh,
        in_specs=(P(), P(), P(), P(), tokens, tokens, tokens, tokens),
        out_specs=(tokens, tokens, tokens, P("mlp", "seq"), P("mlp", "seq"), P("mlp", "seq")),
        check_vma=False,
    )
```

time: 48.9 us -> 44.5 us (0.910)
  Pallas kernels: 48 us -> 43.6 us
    pallas_call x1, Pallas kernels: 47.3 us -> 42.9 us  [per_device(): pl.pallas_call(body, out_shape=[pltpu.VMEM((16, 3, 16, HD), BF), pltpu.VM...]
where the time goes in v3:
time: 44.5 us; the launch traced here: 44.3 us
  Pallas kernels  43.6 us (98%)
  between operations  0.64 us (1%)
    pallas_call x1, Pallas kernels, per_device(): pl.pallas_call(body, out_shape=[pltpu.VMEM((16, 3, 16, HD), BF), pltpu.VM...  42.9 us

profile of v3, /device:TPU:1, one launch (start us, length us, event | category | flops | bytes accessed | tf_op | source)
XLA Modules:
  0.0 44.3 jit_solution(15439461821840497145)
XLA Ops:
  0.6 42.9 %shard_map.127 = (bf16[16,3,16,128]{3,2,1,0:T(8,128)(2,1)S(1)}, bf16[3,32,128]{2,1,0:T(8,128)(2,1)S(1)}) custom-call(bf16[512,2048]{1,0:T(8,128)(2,1)} %tq.1, bf16[512,2048]{1,0:T(8,128)(2,1)} %tk.1, bf16[512,2048]{1,0:T(8,128)(2,1)} %tv.1, bf16[512,2048]{1,0:T(8,128)(2,1)} %tg.1, bf16[16,2048]{1,0:T(8,128)(2,1)} %iq.1, bf16[16,2048]{1,0:T(8,128)(2,1)} %ik.1, ...), custom_call_target="tpu_custom_call" | custom-call | flops 1700000000 | bytes 2000000 | tf_op jit(solution)/shard_map/pallas_call | solution.py:370
  43.5 0.8 %shard_map.128 = (f32[16,2048]{1,0:T(8,128)}, f32[16,2048]{1,0:T(8,128)}, f32[16,2048]{1,0:T(8,128)}, f32[32,128]{1,0:T(8,128)}, f32[32,128]{1,0:T(8,128)}, /*index=5*/f32[32,128]{1,0:T(8,128)}) custom-call(bf16[16,3,16,128]{3,2,1,0:T(8,128)(2,1)S(1)} %get-tuple-element.8.fin, bf16[3,32,128]{2,1,0:T(8,128)(2,1)S(1)} %get-tuple-element.9.tfin), custom_call_target="tpu_custom_call" | custom-call | tf_op jit(solution)/shard_map/pallas_call | solution.py:395

commit v4 on v3

--- a/solution.py
+++ b/solution.py
@@ -39,7 +39,7 @@
     dq_st, dq_in, dq_own, dqt_st, dqt_in, dq_text,
     out_st, tout,
     in_sem, text_sem,
-    p1_s, p1_r, qg_s, qg_r, ql, kv_s, kv_r, st_s, st_r,
+    p1_s, p1_r, qg_s, qg_r, kv_s, kv_r, st_s, st_r,
     dkv_s, dkv_r, dkvt_s, dkvt_r, dq_s, dq_r, dqt_s, dqt_r,
     p4_s, p4_r, tx_s, tx_r,
 ):
@@ -95,38 +95,6 @@
         c = pltpu.make_async_copy(ref, flat.at[n], in_sem.at[n])
         c.start()
         loads.append(c)
-
-    barrier = pltpu.get_barrier_semaphore()
-    def greet(to):
-        pl.semaphore_signal(barrier, inc=1, device_id=to, device_id_type=MESH)
-
-    for i in range(15, 0, -1):
-        greet(column(i, 1))
-
-    @pl.when(y != zh)
-    def _():
-        greet(partner)
-
-    for j in (2, 3, 1):
-        greet(turn(j))
-        greet(shift(j))
-
-    for n, c in enumerate(loads):
-        c.wait()
-        for h in range(16):
-            stage[h, n] = flat[n, :, h * HD:(h + 1) * HD]
-
-    @pl.when(y != zh)
-    def _():
-        pl.semaphore_wait(barrier, 22)
-
-    @pl.when(y == zh)
-    def _():
-        pl.semaphore_wait(barrier, 21)
-
-    for i in range(1, 16):
-        send(stage.at[head_of(i, -1)], own.at[i], p1_s.at[i], p1_r.at[i], column(i, -1))
-    own[0] = stage[head]
 
     col = pl.ds(pl.multiple_of(head * HD, HD), HD)
     tloads = []
@@ -137,12 +105,28 @@
             c = pltpu.make_async_copy(ref.at[rows, col], text.at[n, pl.ds(j * 32, 32)], text_sem.at[n, j])
             c.start()
             tloads.append(c)
-    for c in tloads:
+
+    barrier = pltpu.get_barrier_semaphore()
+    def greet(to):
+        pl.semaphore_signal(barrier, inc=1, device_id=to, device_id_type=MESH)
+
+    for i in range(15, 0, -1):
+        greet(column(i, 1))
+
+    for j in (2, 3, 1):
+        greet(turn(j))
+        greet(shift(j))
+
+    for n, c in enumerate(loads):
         c.wait()
-    qall[0:128] = text[0]
-    gall[0:128] = text[1]
-    kall[0:128] = text[2]
-    vall[0:128] = text[3]
+        for h in range(16):
+            stage[h, n] = flat[n, :, h * HD:(h + 1) * HD]
+
+    pl.semaphore_wait(barrier, 21)
+
+    for i in range(1, 16):
+        send(stage.at[head_of(i, -1)], own.at[i], p1_s.at[i], p1_r.at[i], column(i, -1))
+    own[0] = stage[head]
 
     for i in range(16):
         if i:
@@ -155,7 +139,6 @@
             pltpu.make_async_remote_copy(
                 own.at[i, pl.ds(0, 2)], qg.at[u, i], qg_s.at[j - 1], qg_r.at[u, g],
                 device_id=shift(j), device_id_type=MESH).start()
-        pltpu.make_async_copy(own.at[i, pl.ds(0, 2)], qg.at[u, i], ql.at[g]).start()
 
     def query_rows(qc):
         return pl.ds(START[qc], SIZE[qc])
@@ -184,7 +167,7 @@
             arrive(kv.at[j - 1, slots], kv_r.at[j - 1, g])
             a = (u + 4 - j) % 4
             arrive(qg.at[a, slots], qg_r.at[a, g])
-        arrive(qg.at[u, slots], ql.at[g])
+        qg[u, slots] = own[slots, 0:2]
         for b in range(4):
             r = pl.ds(START[g + 1] + 64 * b, 64)
             k, val = (kv[b - 1, slots, 0], kv[b - 1, slots, 1]) if b else (own[slots, 2], own[slots, 3])
@@ -193,6 +176,12 @@
             qall[r] = qg[b, slots, 0].reshape(64, HD)
             gall[r] = qg[b, slots, 1].reshape(64, HD)
 
+    for c in tloads:
+        c.wait()
+    qall[0:128] = text[0]
+    gall[0:128] = text[1]
+    kall[0:128] = text[2]
+    vall[0:128] = text[3]
     pass_one(0, 0)
     for g in range(4):
         take(g)
@@ -275,7 +264,7 @@
         for j in (2, 1, 3):
             send(dq_st.at[g, (u + 4 - j) % 4], dq_in.at[j - 1, g], dq_s.at[j - 1, g], dq_r.at[j - 1, g], shift(4 - j))
 
-    for g in (3, 2):
+    for g in FAR[:2]:
         for qc in range(5):
             probs(g + 1, qc)
         keys_out(g)
@@ -289,56 +278,74 @@
         dkvt_st[j - 1, 0] = dk[part].astype(BF)
         dkvt_st[j - 1, 1] = dv[part].astype(BF)
         send(dkvt_st.at[j - 1], dkvt_in.at[j - 1], dkvt_s.at[j - 1], dkvt_r.at[j - 1], turn(4 - j))
-    for kc in (2, 1):
-        probs(kc, 0)
+    for g in FAR[2:]:
+        probs(g + 1, 0)
     dq_text[...] = query_grad(0)
     for j in (2, 1, 3):
         dqt_st[j - 1] = dq_text[text_part(j)].astype(BF)
         send(dqt_st.at[j - 1], dqt_in.at[j - 1], dqt_s.at[j - 1], dqt_r.at[j - 1], shift(4 - j))
-    for g in (1, 0):
+    for g in FAR[2:]:
         for qc in range(1, 5):
             probs(g + 1, qc)
         keys_out(g)
     for g in FAR:
         queries_out(g)
 
-    for j in range(3):
-        arrive(dqt_in.at[j], dqt_r.at[j])
-        arrive(dkvt_in.at[j], dkvt_r.at[j])
-
     def plus(own_term, terms):
         for t in terms:
             own_term = own_term + t.astype(F32)
         return own_term
 
-    tout[0] = plus(dq_text[text_part(0)], [dqt_in[j] for j in range(3)]).astype(BF)
-    tout[1] = plus(dkvt_own[0], [dkvt_in[j, 0] for j in range(3)]).astype(BF)
-    tout[2] = plus(dkvt_own[1], [dkvt_in[j, 1] for j in range(3)]).astype(BF)
-    tcopy = pltpu.make_async_remote_copy(
-        tout, tfin, tx_s, tx_r, device_id=partner, device_id_type=MESH)
-
-    @pl.when(y != zh)
-    def _():
-        tcopy.start()
-
-    @pl.when(y == zh)
-    def _():
-        tfin[...] = tout[...]
-
-    for g in FAR:
+    def hand_back(g, part):
+        for i in range(4 * g, 4 * g + 4):
+            if i:
+                at, n, sems = (slice(0, 1), 1, 1) if part else (slice(1, 3), 2, 0)
+                rows = pl.ds(at.start, n)
+                send(out_st.at[i, rows], fin.at[head, rows], p4_s.at[sems, i], p4_r.at[sems, i], column(i, 1))
+
+    def keys_back(g):
         slots = pl.ds(4 * g, 4)
         for j in range(3):
             arrive(dkv_in.at[j, g], dkv_r.at[j, g])
         for n in (0, 1):
             total = plus(dkv_own[g, n], [dkv_in[j, g, n] for j in range(3)])
             out_st[slots, n + 1] = total.astype(BF).reshape(4, 16, HD)
+        hand_back(g, 0)
+
+    def queries_back(g):
+        slots = pl.ds(4 * g, 4)
         for j in range(3):
             arrive(dq_in.at[j, g], dq_r.at[j, g])
         total = plus(dq_own[g, u], [dq_in[j, g] for j in range(3)])
         out_st[slots, 0] = total.astype(BF).reshape(4, 16, HD)
-        for i in range(4 * g, 4 * g + 4):
-            if i:
-                send(out_st.at[i], fin.at[head], p4_s.at[i], p4_r.at[i], column(i, 1))
+        hand_back(g, 1)
+
+    keys_back(FAR[0])
+    keys_back(FAR[1])
+    for j in range(3):
+        arrive(dqt_in.at[j], dqt_r.at[j])
+        arrive(dkvt_in.at[j], dkvt_r.at[j])
+
+    tout[0] = plus(dq_text[text_part(0)], [dqt_in[j] for j in range(3)]).astype(BF)
+    tout[1] = plus(dkvt_own[0], [dkvt_in[j, 0] for j in range(3)]).astype(BF)
+    tout[2] = plus(dkvt_own[1], [dkvt_in[j, 1] for j in range(3)]).astype(BF)
+    tcopy = pltpu.make_async_remote_copy(
+        tout, tfin, tx_s, tx_r, device_id=partner, device_id_type=MESH)
+
+    @pl.when(y != zh)
+    def _():
+        tcopy.start()
+
+    @pl.when(y == zh)
+    def _():
+        tfin[...] = tout[...]
+
+    keys_back(FAR[2])
+    queries_back(FAR[0])
+    keys_back(FAR[3])
+    queries_back(FAR[1])
+    queries_back(FAR[2])
+    queries_back(FAR[3])
     fin[head] = out_st[0]
 
     for j in range(3):
@@ -347,7 +354,9 @@
     for c in sends:
         c.wait_send()
     for i in range(15, 0, -1):
-        arrive(fin.at[head_of(i, -1)], p4_r.at[i])
+        there = head_of(i, -1)
+        arrive(fin.at[there, pl.ds(1, 2)], p4_r.at[0, i])
+        arrive(fin.at[there, pl.ds(0, 1)], p4_r.at[1, i])
 
     @pl.when(y != zh)
     def _():
@@ -384,9 +393,9 @@
             V((3, 32, HD), BF), V((3, 32, HD), BF), V((HD, HD), F32),
             V((16, 3, 16, HD), BF), V((3, 32, HD), BF),
             sem((4,)), sem((4, 4)),
-            sem((16,)), sem((16,)), sem((3,)), sem((4, 4)), sem((4,)), sem((3,)), sem((3, 4)), sem((3,)), sem((3,)),
+            sem((16,)), sem((16,)), sem((3,)), sem((4, 4)), sem((3,)), sem((3, 4)), sem((3,)), sem((3,)),
             sem((3, 4)), sem((3, 4)), sem((3,)), sem((3,)), sem((3, 4)), sem((3, 4)), sem((3,)), sem((3,)),
-            sem((16,)), sem((16,)), sem, sem,
+            sem((2, 16)), sem((2, 16)), sem, sem,
         ],
         compiler_params=pltpu.CompilerParams(
             collective_id=0, has_side_effects=True, vmem_limit_bytes=48 * 1024 * 1024),

time: 44.5 us -> 43.5 us (0.978)
  Pallas kernels: 43.6 us -> 42.8 us
    pallas_call x1, Pallas kernels: 42.9 us -> 42 us  [per_device(): pl.pallas_call(body, out_shape=[pltpu.VMEM((16, 3, 16, HD), BF), pltpu.VM...]
where the time goes in v4:
time: 43.5 us; the launch traced here: 43.4 us
  Pallas kernels  42.8 us (98%)
  between operations  0.64 us (1%)
    pallas_call x1, Pallas kernels, per_device(): pl.pallas_call(body, out_shape=[pltpu.VMEM((16, 3, 16, HD), BF), pltpu.VM...  42 us

profile of v4, /device:TPU:1, one launch (start us, length us, event | category | flops | bytes accessed | tf_op | source)
XLA Modules:
  0.0 43.4 jit_solution(3453958965131504822)
XLA Ops:
  0.6 42.0 %shard_map.127 = (bf16[16,3,16,128]{3,2,1,0:T(8,128)(2,1)S(1)}, bf16[3,32,128]{2,1,0:T(8,128)(2,1)S(1)}) custom-call(bf16[512,2048]{1,0:T(8,128)(2,1)} %tq.1, bf16[512,2048]{1,0:T(8,128)(2,1)} %tk.1, bf16[512,2048]{1,0:T(8,128)(2,1)} %tv.1, bf16[512,2048]{1,0:T(8,128)(2,1)} %tg.1, bf16[16,2048]{1,0:T(8,128)(2,1)} %iq.1, bf16[16,2048]{1,0:T(8,128)(2,1)} %ik.1, ...), custom_call_target="tpu_custom_call" | custom-call | flops 1700000000 | bytes 2000000 | tf_op jit(solution)/shard_map/pallas_call | solution.py:379
  42.6 0.8 %shard_map.128 = (f32[16,2048]{1,0:T(8,128)}, f32[16,2048]{1,0:T(8,128)}, f32[16,2048]{1,0:T(8,128)}, f32[32,128]{1,0:T(8,128)}, f32[32,128]{1,0:T(8,128)}, /*index=5*/f32[32,128]{1,0:T(8,128)}) custom-call(bf16[16,3,16,128]{3,2,1,0:T(8,128)(2,1)S(1)} %get-tuple-element.8.fin, bf16[3,32,128]{2,1,0:T(8,128)(2,1)S(1)} %get-tuple-element.9.tfin), custom_call_target="tpu_custom_call" | custom-call | tf_op jit(solution)/shard_map/pallas_call | solution.py:404

commit v5 on v4

--- a/solution.py
+++ b/solution.py
@@ -39,7 +39,7 @@
     dq_st, dq_in, dq_own, dqt_st, dqt_in, dq_text,
     out_st, tout,
     in_sem, text_sem,
-    p1_s, p1_r, qg_s, qg_r, kv_s, kv_r, st_s, st_r,
+    p1_s, p1_r, qg_s, kv_s, p2_r, st_s, st_r,
     dkv_s, dkv_r, dkvt_s, dkvt_r, dq_s, dq_r, dqt_s, dqt_r,
     p4_s, p4_r, tx_s, tx_r,
 ):
@@ -80,65 +80,51 @@
         return zo * 8 + zi * 2 + other
 
     partner = {"seq": z0 * 8 + zh * 2 + core, "mlp": x * 4 + y}
-    sends = []
-
     def send(src, dst, ss, rs, to):
-        c = pltpu.make_async_remote_copy(src, dst, ss, rs, device_id=to, device_id_type=MESH)
-        c.start()
-        sends.append(c)
+        pltpu.make_async_remote_copy(src, dst, ss, rs, device_id=to, device_id_type=MESH).start()
 
     def arrive(ref, sem):
         pltpu.make_async_copy(ref, ref, sem).wait()
 
-    loads = []
     for n, ref in enumerate((iq, ig, ik, iv)):
-        c = pltpu.make_async_copy(ref, flat.at[n], in_sem.at[n])
-        c.start()
-        loads.append(c)
+        pltpu.make_async_copy(ref, flat.at[n], in_sem).start()
+
+    barrier = pltpu.get_barrier_semaphore()
+    def greet(to):
+        pl.semaphore_signal(barrier, inc=1, device_id=to, device_id_type=MESH)
+
+    for i in range(15, 0, -1):
+        greet(column(i, 1))
+
+    for j in (2, 3, 1):
+        greet(turn(j))
+        greet(shift(j))
 
     col = pl.ds(pl.multiple_of(head * HD, HD), HD)
-    tloads = []
     for n, ref in enumerate((tq, tg, tk, tv)):
         for j in range(4):
             owner = block(j, v) if n < 2 else block(u, (v + 4 - j) % 4)
             rows = pl.ds(pl.multiple_of(owner * 32, 32), 32)
-            c = pltpu.make_async_copy(ref.at[rows, col], text.at[n, pl.ds(j * 32, 32)], text_sem.at[n, j])
-            c.start()
-            tloads.append(c)
-
-    barrier = pltpu.get_barrier_semaphore()
-    def greet(to):
-        pl.semaphore_signal(barrier, inc=1, device_id=to, device_id_type=MESH)
-
-    for i in range(15, 0, -1):
-        greet(column(i, 1))
-
-    for j in (2, 3, 1):
-        greet(turn(j))
-        greet(shift(j))
-
-    for n, c in enumerate(loads):
-        c.wait()
+            pltpu.make_async_copy(ref.at[rows, col], text.at[n, pl.ds(j * 32, 32)], text_sem).start()
+
+    arrive(flat, in_sem)
+    for n in range(4):
         for h in range(16):
             stage[h, n] = flat[n, :, h * HD:(h + 1) * HD]
 
     pl.semaphore_wait(barrier, 21)
 
     for i in range(1, 16):
-        send(stage.at[head_of(i, -1)], own.at[i], p1_s.at[i], p1_r.at[i], column(i, -1))
+        send(stage.at[head_of(i, -1)], own.at[i], p1_s, p1_r.at[i - 1], column(i, -1))
     own[0] = stage[head]
 
     for i in range(16):
         if i:
-            arrive(own.at[i], p1_r.at[i])
+            arrive(own.at[i], p1_r.at[i - 1])
         g = i // 4
         for j in (2, 1, 3):
-            pltpu.make_async_remote_copy(
-                own.at[i, pl.ds(2, 2)], kv.at[j - 1, i], kv_s.at[j - 1], kv_r.at[j - 1, g],
-                device_id=turn(j), device_id_type=MESH).start()
-            pltpu.make_async_remote_copy(
-                own.at[i, pl.ds(0, 2)], qg.at[u, i], qg_s.at[j - 1], qg_r.at[u, g],
-                device_id=shift(j), device_id_type=MESH).start()
+            send(own.at[i, pl.ds(2, 2)], kv.at[j - 1, i], kv_s, p2_r.at[g], turn(j))
+            send(own.at[i, pl.ds(0, 2)], qg.at[u, i], qg_s, p2_r.at[g], shift(j))
 
     def query_rows(qc):
         return pl.ds(START[qc], SIZE[qc])
@@ -163,10 +149,7 @@
 
     def take(g):
         slots = pl.ds(4 * g, 4)
-        for j in range(1, 4):
-            arrive(kv.at[j - 1, slots], kv_r.at[j - 1, g])
-            a = (u + 4 - j) % 4
-            arrive(qg.at[a, slots], qg_r.at[a, g])
+        arrive(own.at[pl.ds(0, 12)], p2_r.at[g])
         qg[u, slots] = own[slots, 0:2]
         for b in range(4):
             r = pl.ds(START[g + 1] + 64 * b, 64)
@@ -176,8 +159,7 @@
             qall[r] = qg[b, slots, 0].reshape(64, HD)
             gall[r] = qg[b, slots, 1].reshape(64, HD)
 
-    for c in tloads:
-        c.wait()
+    arrive(text, text_sem)
     qall[0:128] = text[0]
     gall[0:128] = text[1]
     kall[0:128] = text[2]
@@ -204,10 +186,9 @@
                 b = 2 * qc - 1 + half if qc else 0
                 st[i * 9 + b:i * 9 + b + 1] = row[:, half * 128:(half + 1) * 128]
     for j in (2, 3, 1):
-        send(st, st_in.at[j - 1], st_s.at[j - 1], st_r.at[j - 1], shift(j))
+        send(st, st_in.at[j - 1], st_s, st_r, shift(j))
     ktall[...] = kall[...].T
-    for j in (1, 2, 3):
-        arrive(st_in.at[j - 1], st_r.at[j - 1])
+    arrive(st_in, st_r)
 
     tops, sums, dsums = ([st[n:n + 9]] + [st_in[j, n:n + 9] for j in range(3)] for n in (0, 9, 18))
     gtop = jnp.maximum(jnp.maximum(tops[0], tops[1]), jnp.maximum(tops[2], tops[3]))
@@ -255,14 +236,14 @@
         for j in (2, 1, 3):
             dkv_st[j - 1, g, 0] = dk[64 * j:64 * j + 64].astype(BF)
             dkv_st[j - 1, g, 1] = dv[64 * j:64 * j + 64].astype(BF)
-            send(dkv_st.at[j - 1, g], dkv_in.at[j - 1, g], dkv_s.at[j - 1, g], dkv_r.at[j - 1, g], turn(4 - j))
+            send(dkv_st.at[j - 1, g], dkv_in.at[j - 1, g], dkv_s, dkv_r.at[g], turn(4 - j))
 
     def queries_out(g):
         dq = query_grad(g + 1).reshape(4, 64, HD)
         dq_own[g] = dq
         dq_st[g] = dq.astype(BF)
         for j in (2, 1, 3):
-            send(dq_st.at[g, (u + 4 - j) % 4], dq_in.at[j - 1, g], dq_s.at[j - 1, g], dq_r.at[j - 1, g], shift(4 - j))
+            send(dq_st.at[g, (u + 4 - j) % 4], dq_in.at[j - 1, g], dq_s, dq_r.at[g], shift(4 - j))
 
     for g in FAR[:2]:
         for qc in range(5):
@@ -277,13 +258,13 @@
         part = slice(j * 32, j * 32 + 32)
         dkvt_st[j - 1, 0] = dk[part].astype(BF)
         dkvt_st[j - 1, 1] = dv[part].astype(BF)
-        send(dkvt_st.at[j - 1], dkvt_in.at[j - 1], dkvt_s.at[j - 1], dkvt_r.at[j - 1], turn(4 - j))
+        send(dkvt_st.at[j - 1], dkvt_in.at[j - 1], dkvt_s, dkvt_r, turn(4 - j))
     for g in FAR[2:]:
         probs(g + 1, 0)
     dq_text[...] = query_grad(0)
     for j in (2, 1, 3):
         dqt_st[j - 1] = dq_text[text_part(j)].astype(BF)
-        send(dqt_st.at[j - 1], dqt_in.at[j - 1], dqt_s.at[j - 1], dqt_r.at[j - 1], shift(4 - j))
+        send(dqt_st.at[j - 1], dqt_in.at[j - 1], dqt_s, dqt_r, shift(4 - j))
     for g in FAR[2:]:
         for qc in range(1, 5):
             probs(g + 1, qc)
@@ -299,14 +280,13 @@
     def hand_back(g, part):
         for i in range(4 * g, 4 * g + 4):
             if i:
-                at, n, sems = (slice(0, 1), 1, 1) if part else (slice(1, 3), 2, 0)
-                rows = pl.ds(at.start, n)
-                send(out_st.at[i, rows], fin.at[head, rows], p4_s.at[sems, i], p4_r.at[sems, i], column(i, 1))
+                at, n = (0, 1) if part else (1, 2)
+                rows = pl.ds(at, n)
+                send(out_st.at[i, rows], fin.at[head, rows], p4_s, p4_r, column(i, 1))
 
     def keys_back(g):
         slots = pl.ds(4 * g, 4)
-        for j in range(3):
-            arrive(dkv_in.at[j, g], dkv_r.at[j, g])
+        arrive(dkv_in.at[:, g], dkv_r.at[g])
         for n in (0, 1):
             total = plus(dkv_own[g, n], [dkv_in[j, g, n] for j in range(3)])
             out_st[slots, n + 1] = total.astype(BF).reshape(4, 16, HD)
@@ -314,17 +294,15 @@
 
     def queries_back(g):
         slots = pl.ds(4 * g, 4)
-        for j in range(3):
-            arrive(dq_in.at[j, g], dq_r.at[j, g])
+        arrive(dq_in.at[:, g], dq_r.at[g])
         total = plus(dq_own[g, u], [dq_in[j, g] for j in range(3)])
         out_st[slots, 0] = total.astype(BF).reshape(4, 16, HD)
         hand_back(g, 1)
 
     keys_back(FAR[0])
     keys_back(FAR[1])
-    for j in range(3):
-        arrive(dqt_in.at[j], dqt_r.at[j])
-        arrive(dkvt_in.at[j], dkvt_r.at[j])
+    arrive(dqt_in, dqt_r)
+    arrive(dkvt_in, dkvt_r)
 
     tout[0] = plus(dq_text[text_part(0)], [dqt_in[j] for j in range(3)]).astype(BF)
     tout[1] = plus(dkvt_own[0], [dkvt_in[j, 0] for j in range(3)]).astype(BF)
@@ -348,15 +326,16 @@
     queries_back(FAR[3])
     fin[head] = out_st[0]
 
-    for j in range(3):
-        arrive(kv.at[j], kv_s.at[j])
-        arrive(kv.at[j], qg_s.at[j])
-    for c in sends:
-        c.wait_send()
-    for i in range(15, 0, -1):
-        there = head_of(i, -1)
-        arrive(fin.at[there, pl.ds(1, 2)], p4_r.at[0, i])
-        arrive(fin.at[there, pl.ds(0, 1)], p4_r.at[1, i])
+    arrive(own.at[pl.ds(0, 15)], p1_s)
+    arrive(kv, kv_s)
+    arrive(kv, qg_s)
+    arrive(st_in, st_s)
+    arrive(dkv_st, dkv_s)
+    arrive(dq_in, dq_s)
+    arrive(dkvt_st, dkvt_s)
+    arrive(dqt_st, dqt_s)
+    arrive(fin.at[pl.ds(0, 15)], p4_s)
+    arrive(fin.at[pl.ds(0, 15)], p4_r)
 
     @pl.when(y != zh)
     def _():
@@ -392,10 +371,10 @@
             V((4, 4, 64, HD), BF), V((3, 4, 64, HD), BF), V((4, 4, 64, HD), F32),
             V((3, 32, HD), BF), V((3, 32, HD), BF), V((HD, HD), F32),
             V((16, 3, 16, HD), BF), V((3, 32, HD), BF),
-            sem((4,)), sem((4, 4)),
-            sem((16,)), sem((16,)), sem((3,)), sem((4, 4)), sem((3,)), sem((3, 4)), sem((3,)), sem((3,)),
-            sem((3, 4)), sem((3, 4)), sem((3,)), sem((3,)), sem((3, 4)), sem((3, 4)), sem((3,)), sem((3,)),
-            sem((2, 16)), sem((2, 16)), sem, sem,
+            sem, sem,
+            sem, sem((15,)), sem, sem, sem((4,)), sem, sem,
+            sem, sem((4,)), sem, sem, sem, sem((4,)), sem, sem,
+            sem, sem, sem, sem,
         ],
         compiler_params=pltpu.CompilerParams(
             collective_id=0, has_side_effects=True, vmem_limit_bytes=48 * 1024 * 1024),

time: 43.5 us -> 41.9 us (0.963)
  Pallas kernels: 42.8 us -> 41.1 us
    pallas_call x1, Pallas kernels: 42 us -> 40.4 us  [per_device(): pl.pallas_call(body, out_shape=[pltpu.VMEM((16, 3, 16, HD), BF), pltpu.VM...]
where the time goes in v5:
time: 41.9 us; the launch traced here: 41.8 us
  Pallas kernels  41.1 us (98%)
  between operations  0.64 us (2%)
    pallas_call x1, Pallas kernels, per_device(): pl.pallas_call(body, out_shape=[pltpu.VMEM((16, 3, 16, HD), BF), pltpu.VM...  40.4 us

profile of v5, /device:TPU:1, one launch (start us, length us, event | category | flops | bytes accessed | tf_op | source)
XLA Modules:
  0.0 41.8 jit_solution(8334751069530126032)
XLA Ops:
  0.6 40.4 %shard_map.127 = (bf16[16,3,16,128]{3,2,1,0:T(8,128)(2,1)S(1)}, bf16[3,32,128]{2,1,0:T(8,128)(2,1)S(1)}) custom-call(bf16[512,2048]{1,0:T(8,128)(2,1)} %tq.1, bf16[512,2048]{1,0:T(8,128)(2,1)} %tk.1, bf16[512,2048]{1,0:T(8,128)(2,1)} %tv.1, bf16[512,2048]{1,0:T(8,128)(2,1)} %tg.1, bf16[16,2048]{1,0:T(8,128)(2,1)} %iq.1, bf16[16,2048]{1,0:T(8,128)(2,1)} %ik.1, ...), custom_call_target="tpu_custom_call" | custom-call | flops 1700000000 | bytes 2000000 | tf_op jit(solution)/shard_map/pallas_call | solution.py:358
  41.0 0.8 %shard_map.128 = (f32[16,2048]{1,0:T(8,128)}, f32[16,2048]{1,0:T(8,128)}, f32[16,2048]{1,0:T(8,128)}, f32[32,128]{1,0:T(8,128)}, f32[32,128]{1,0:T(8,128)}, /*index=5*/f32[32,128]{1,0:T(8,128)}) custom-call(bf16[16,3,16,128]{3,2,1,0:T(8,128)(2,1)S(1)} %get-tuple-element.8.fin, bf16[3,32,128]{2,1,0:T(8,128)(2,1)S(1)} %get-tuple-element.9.tfin), custom_call_target="tpu_custom_call" | custom-call | tf_op jit(solution)/shard_map/pallas_call | solution.py:383

commit v6 on v5

--- a/solution.py
+++ b/solution.py
@@ -245,7 +245,7 @@
         for j in (2, 1, 3):
             send(dq_st.at[g, (u + 4 - j) % 4], dq_in.at[j - 1, g], dq_s, dq_r.at[g], shift(4 - j))
 
-    for g in FAR[:2]:
+    for g in FAR[:1]:
         for qc in range(5):
             probs(g + 1, qc)
         keys_out(g)
@@ -259,13 +259,13 @@
         dkvt_st[j - 1, 0] = dk[part].astype(BF)
         dkvt_st[j - 1, 1] = dv[part].astype(BF)
         send(dkvt_st.at[j - 1], dkvt_in.at[j - 1], dkvt_s, dkvt_r, turn(4 - j))
-    for g in FAR[2:]:
+    for g in FAR[1:]:
         probs(g + 1, 0)
     dq_text[...] = query_grad(0)
     for j in (2, 1, 3):
         dqt_st[j - 1] = dq_text[text_part(j)].astype(BF)
         send(dqt_st.at[j - 1], dqt_in.at[j - 1], dqt_s, dqt_r, shift(4 - j))
-    for g in FAR[2:]:
+    for g in FAR[1:]:
         for qc in range(1, 5):
             probs(g + 1, qc)
         keys_out(g)
@@ -299,8 +299,6 @@
         out_st[slots, 0] = total.astype(BF).reshape(4, 16, HD)
         hand_back(g, 1)
 
-    keys_back(FAR[0])
-    keys_back(FAR[1])
     arrive(dqt_in, dqt_r)
     arrive(dkvt_in, dkvt_r)
 
@@ -318,6 +316,8 @@
     def _():
         tfin[...] = tout[...]
 
+    keys_back(FAR[0])
+    keys_back(FAR[1])
     keys_back(FAR[2])
     queries_back(FAR[0])
     keys_back(FAR[3])

time: 41.9 us -> 41.8 us (level)
  no operation moved by 1% of the time
where the time goes in v6:
time: 41.8 us; the launch traced here: 41.7 us
  Pallas kernels  41 us (98%)
  between operations  0.64 us (2%)
    pallas_call x1, Pallas kernels, per_device(): pl.pallas_call(body, out_shape=[pltpu.VMEM((16, 3, 16, HD), BF), pltpu.VM...  40.3 us

profile of v6, /device:TPU:1, one launch (start us, length us, event | category | flops | bytes accessed | tf_op | source)
XLA Modules:
  0.0 41.7 jit_solution(14659393220269791130)
XLA Ops:
  0.6 40.3 %shard_map.127 = (bf16[16,3,16,128]{3,2,1,0:T(8,128)(2,1)S(1)}, bf16[3,32,128]{2,1,0:T(8,128)(2,1)S(1)}) custom-call(bf16[512,2048]{1,0:T(8,128)(2,1)} %tq.1, bf16[512,2048]{1,0:T(8,128)(2,1)} %tk.1, bf16[512,2048]{1,0:T(8,128)(2,1)} %tv.1, bf16[512,2048]{1,0:T(8,128)(2,1)} %tg.1, bf16[16,2048]{1,0:T(8,128)(2,1)} %iq.1, bf16[16,2048]{1,0:T(8,128)(2,1)} %ik.1, ...), custom_call_target="tpu_custom_call" | custom-call | flops 1700000000 | bytes 2000000 | tf_op jit(solution)/shard_map/pallas_call | solution.py:358
  40.9 0.8 %shard_map.128 = (f32[16,2048]{1,0:T(8,128)}, f32[16,2048]{1,0:T(8,128)}, f32[16,2048]{1,0:T(8,128)}, f32[32,128]{1,0:T(8,128)}, f32[32,128]{1,0:T(8,128)}, /*index=5*/f32[32,128]{1,0:T(8,128)}) custom-call(bf16[16,3,16,128]{3,2,1,0:T(8,128)(2,1)S(1)} %get-tuple-element.8.fin, bf16[3,32,128]{2,1,0:T(8,128)(2,1)S(1)} %get-tuple-element.9.tfin), custom_call_target="tpu_custom_call" | custom-call | tf_op jit(solution)/shard_map/pallas_call | solution.py:383
